TPU v7x, 256 devices: a whole 4x4x8 slice. The times are simulated.
256 devices in a mesh: wide: 64 (over z, x, core), narrow: 4 (over y).
Axes of the slice: x: 4, y: 4, z: 8, core: 2. Of those that a mesh axis runs over, the one named last changes fastest.
Arguments:
- tokens: bfloat16 [32768, 4096], P('wide', 'narrow'), may hold values from -6 to 6
- cotangent: bfloat16 [32768, 1024], P('wide', 'narrow'), may hold values from -6 to 6
- frozen_key_weight: bfloat16 [4096, 1024], P(None, 'narrow'), may hold values from -0.1875 to 0.1875
- adapter_down_maps: bfloat16 [512, 64, 4096], P('wide', None, 'narrow'), may hold values from -0.09375 to 0.09375
- adapter_up_maps: bfloat16 [512, 64, 1024], P('wide', None, 'narrow'), may hold values from -0.1875 to 0.1875
- previous_down_maps: bfloat16 [512, 64, 4096], P('wide', None, 'narrow'), may hold values from -0.09375 to 0.09375
- previous_up_maps: bfloat16 [512, 64, 1024], P('wide', None, 'narrow'), may hold values from -0.1875 to 0.1875
- down_fisher_diagonal: float32 [512, 64, 4096], P('wide', None, 'narrow'), may hold values from 1 to 30
- up_fisher_diagonal: float32 [512, 64, 1024], P('wide', None, 'narrow'), may hold values from 1 to 30
- token_adapter_index: int32 [32768], P('wide'), may hold values from 0 to 511, as said below
Outputs:
- layer_input_gradient: bfloat16 [32768, 4096], P('wide', 'narrow')
- down_map_gradient: float32 [512, 64, 4096], P('wide', None, 'narrow')
- up_map_gradient: float32 [512, 64, 1024], P('wide', None, 'narrow')
Inputs may be any that keep to these rules, and one draw needn't show every extreme that they name: `token_adapter_index`: adapters a with equal a // 8 share one owner. In every aligned block of 512 tokens one owner, the same in all blocks, is named by exactly 24 tokens, a second owner by exactly 10, and every other owner by at most 10.
All inputs are finite; a program needn't handle non-finite values.
Results may differ from a plain program's by a relative error of at most 0.0059.
Values may be sent and summed in bfloat16 or wider, within the bound.
A program may use at most 128 MiB of HBM per device.

v0:
```python
import jax
import jax.numpy as jnp
from jax import lax
from jax.sharding import PartitionSpec as P

adapter_scale = 2.0
anchor_penalty_weight = 20.0


def on_device(
    tokens,
    cotangent,
    frozen_key_weight,
    adapter_down_maps,
    adapter_up_maps,
    previous_down_maps,
    previous_up_maps,
    down_fisher_diagonal,
    up_fisher_diagonal,
    token_adapter_index,
):
    tenant_list = lax.axis_size("wide")
    tok_count = tokens.shape[0]
    tenant_adapters = 3 * (tok_count // tenant_list)
    tenant_slot_count = tenant_list * tenant_adapters
    grouped_adapters = adapter_down_maps.shape[0]
    reduced_projection = adapter_down_maps.shape[1]
    contract_last = (((1,), (1,)), ((), ()))
    contract_first = (((0,), (0,)), ((), ()))
    owner_of = token_adapter_index // grouped_adapters
    local_id = token_adapter_index % grouped_adapters
    member = (owner_of[:, None] == jnp.arange(tenant_list, dtype=jnp.int32)[None, :]).astype(
        jnp.int32
    )
    position = jnp.sum(jnp.cumsum(member, axis=0) * member, axis=1) - 1
    slot_lookup = owner_of * tenant_adapters + position
    source = (
        jnp.zeros((tenant_slot_count,), jnp.int32)
        .at[slot_lookup]
        .set(jnp.arange(tok_count, dtype=jnp.int32))
    )
    filled = jnp.zeros((tenant_slot_count,), jnp.bool_).at[slot_lookup].set(True)
    send_x = jnp.where(filled[:, None], tokens[source], jnp.zeros((), tokens.dtype)).reshape(
        tenant_list, tenant_adapters, -1
    )
    send_dy = jnp.where(filled[:, None], cotangent[source], jnp.zeros((), cotangent.dtype)).reshape(
        tenant_list, tenant_adapters, -1
    )
    send_id = jnp.where(filled, local_id[source], -1).reshape(tenant_list, tenant_adapters)
    recv_x, recv_dy, recv_id = (
        lax.all_to_all(send_x, "wide", split_axis=0, concat_axis=0, tiled=True),
        lax.all_to_all(send_dy, "wide", split_axis=0, concat_axis=0, tiled=True),
        lax.all_to_all(send_id, "wide", split_axis=0, concat_axis=0, tiled=True),
    )
    rows_x = recv_x.reshape(tenant_slot_count, -1)
    rows_dy = recv_dy.reshape(tenant_slot_count, -1)
    flattened_down_maps = adapter_down_maps.reshape(grouped_adapters * reduced_projection, -1)
    flattened_up_maps = adapter_up_maps.reshape(grouped_adapters * reduced_projection, -1)
    selector = (
        recv_id.reshape(tenant_slot_count)[:, None]
        == jnp.arange(grouped_adapters, dtype=jnp.int32)[None, :]
    ).astype(jnp.float32)
    u_every = lax.dot_general(
        rows_x, flattened_down_maps, contract_last, preferred_element_type=jnp.float32
    )
    g_every = lax.dot_general(
        rows_dy, flattened_up_maps, contract_last, preferred_element_type=jnp.float32
    )
    u_part = jnp.sum(
        u_every.reshape(tenant_slot_count, grouped_adapters, reduced_projection)
        * selector[:, :, None],
        axis=1,
    )
    g_part = jnp.sum(
        g_every.reshape(tenant_slot_count, grouped_adapters, reduced_projection)
        * selector[:, :, None],
        axis=1,
    )
    summed = lax.psum(jnp.concatenate([u_part, g_part], axis=1), "narrow")
    u_low = summed[:, :reduced_projection].astype(jnp.bfloat16)
    g_low = summed[:, reduced_projection:].astype(jnp.bfloat16)
    pick_mask = selector.astype(jnp.bfloat16)
    gradient_spread = (pick_mask[:, :, None] * g_low[:, None, :]).reshape(
        tenant_slot_count, grouped_adapters * reduced_projection
    )
    u_spread = (pick_mask[:, :, None] * u_low[:, None, :]).reshape(
        tenant_slot_count, grouped_adapters * reduced_projection
    )
    adapter_row_product = (
        adapter_scale
        * jnp.dot(gradient_spread, flattened_down_maps, preferred_element_type=jnp.float32)
    ).astype(jnp.bfloat16)
    result_tuple = lax.all_to_all(
        adapter_row_product.reshape(tenant_list, tenant_adapters, -1),
        "wide",
        split_axis=0,
        concat_axis=0,
        tiled=True,
    )
    down_data_gradient = lax.dot_general(
        gradient_spread, rows_x, contract_first, preferred_element_type=jnp.float32
    ).reshape(adapter_down_maps.shape)
    up_data_gradient = lax.dot_general(
        u_spread, rows_dy, contract_first, preferred_element_type=jnp.float32
    ).reshape(adapter_up_maps.shape)
    down_map_gradient = (
        adapter_scale * down_data_gradient
        + anchor_penalty_weight
        * down_fisher_diagonal
        * (adapter_down_maps.astype(jnp.float32) - previous_down_maps.astype(jnp.float32))
    )
    up_map_gradient = (
        adapter_scale * up_data_gradient
        + anchor_penalty_weight
        * up_fisher_diagonal
        * (adapter_up_maps.astype(jnp.float32) - previous_up_maps.astype(jnp.float32))
    )
    partial_grad = lax.dot_general(
        cotangent, frozen_key_weight, contract_last, preferred_element_type=jnp.float32
    )
    frozen_contribution = lax.psum_scatter(partial_grad, "narrow", scatter_dimension=1, tiled=True)
    adapter_token_rows = result_tuple.reshape(tenant_slot_count, -1)[slot_lookup]
    layer_input_gradient = (frozen_contribution + adapter_token_rows.astype(jnp.float32)).astype(
        jnp.bfloat16
    )
    return (layer_input_gradient, down_map_gradient, up_map_gradient)


def solution(mesh):
    in_specs = (
        P("wide", "narrow"),
        P("wide", "narrow"),
        P(None, "narrow"),
        P("wide", None, "narrow"),
        P("wide", None, "narrow"),
        P("wide", None, "narrow"),
        P("wide", None, "narrow"),
        P("wide", None, "narrow"),
        P("wide", None, "narrow"),
        P("wide"),
    )
    out_specs = (P("wide", "narrow"), P("wide", None, "narrow"), P("wide", None, "narrow"))
    return jax.shard_map(
        on_device, mesh=mesh, in_specs=in_specs, out_specs=out_specs, check_vma=False
    )
```

profile of v0, /device:TPU:1, one launch (start us, length us, event | category | flops | bytes accessed | tf_op | source)
XLA Modules:
  0.0 293.9 jit_solution(6674999341416400133)
XLA Ops:
  7.2 0.0 copy-start
  7.2 0.0 reduce-scatter.2.cloned.1.call-start
  7.2 1.5 copy-done
  8.8 5.5 %fusion.29 = f32[512,4096]{1,0:T(8,128)} fusion(bf16[512,256]{1,0:T(8,128)(2,1)} %param.11, bf16[4096,256]{1,0:T(8,128)(2,1)S(1)} %copy-done), kind=kOutput, calls=%fused_computation.58 | convolution fusion | flops 1073741824 | bytes 10747904 | tf_op jit(solution)/shard_map/dot_general | solution.py:118
  14.2 0.0 copy-start.3
  14.2 0.0 reduce-scatter.2.cloned.1.call-update
  14.2 0.7 copy-done.3
  14.9 1.2 reduce-window.6
  16.1 0.2 slice_reduce_fusion
  16.4 0.1 fusion.19
  16.6 2.5 scatter_custom_fusion.1
  19.1 2.4 scatter_custom_fusion
  21.5 0.0 copy-start.2
  21.5 9.5 %gather_fusion = s32[1536]{0:T(1024)S(1)} fusion(s32[512]{0:T(512)S(1)} %get-tuple-element.7, s32[2048]{0:T(1024)S(1)} %pad_clamp_fusion), kind=kCustom, calls=%fused_computation | custom fusion | bytes 18432 | tf_op jit(solution)/shard_map/gather | solution.py:49
  31.0 0.7 all_to_all.15
  31.7 13.0 %all-to-all-start = ((s32[64,1,24]{2,1,0:T(1,128)}), s32[64,1,24]{2,1,0:T(1,128)S(1)}, u32[]{:S(2)}, u32[]{:S(2)}) async-start(s32[64,1,24]{2,1,0:T(1,128)} %bitcast.2), calls=%async_computation.1 | async-start | bytes 65536 | tf_op jit(solution)/shard_map/all_to_all | solution.py:53
  44.7 0.0 copy-done.2
  44.7 5.4 %gather_fusion.2 = bf16[1536,256]{1,0:T(8,128)(2,1)} fusion(bf16[512,256]{1,0:T(8,128)(2,1)S(1)} %copy-done.2, s32[2048]{0:T(1024)S(1)} %pad_clamp_fusion), kind=kCustom, calls=%fused_computation.2 | custom fusion | bytes 1579008 | tf_op jit(solution)/shard_map/gather | solution.py:46
  50.1 0.0 copy-start.1
  50.1 0.1 broadcast_in_dim.62
  50.2 2.4 broadcast_select_fusion.1
  52.6 1.4 all-to-all-done
  54.0 9.0 %all-to-all-start.2 = ((bf16[64,24,256]{2,1,0:T(8,128)(2,1)}), bf16[64,24,256]{2,1,0:T(8,128)(2,1)}, u32[]{:S(2)}, u32[]{:S(2)}) async-start(bf16[64,24,256]{2,1,0:T(8,128)(2,1)} %broadcast_select_fusion.1), calls=%async_computation.3 | async-start | bytes 1572864 | tf_op jit(solution)/shard_map/all_to_all | solution.py:52
  63.0 0.0 copy-done.1
  63.0 5.9 %gather_fusion.1 = bf16[1536,1024]{1,0:T(8,128)(2,1)} fusion(bf16[512,1024]{1,0:T(8,128)(2,1)S(1)} %copy-done.1, s32[2048]{0:T(1024)S(1)} %pad_clamp_fusion), kind=kCustom, calls=%fused_computation.1 | custom fusion | bytes 6297600 | tf_op jit(solution)/shard_map/gather | solution.py:43
  68.9 3.3 %broadcast_select_fusion = bf16[64,24,1024]{2,1,0:T(8,128)(2,1)} fusion(bf16[64,24,1024]{2,1,0:T(8,128)(2,1)} %bitcast.58, pred[64,24]{1,0:T(8,128)(4,1)S(1)} %broadcast_in_dim.62), kind=kLoop, calls=%fused_computation.10 | loop fusion | flops 1572864 | bytes 6292992 | tf_op jit(solution)/shard_map/jit(_where)/select_n | solution.py:43
  72.3 0.0 copy-start.7
  72.3 13.5 %all-to-all-done.2 = bf16[64,24,256]{2,1,0:T(8,128)(2,1)} async-done(((bf16[64,24,256]{2,1,0:T(8,128)(2,1)}), bf16[64,24,256]{2,1,0:T(8,128)(2,1)}, u32[]{:S(2)}, u32[]{:S(2)}) %all-to-all-start.2) | async-done | bytes 786464 | tf_op jit(solution)/shard_map/all_to_all | solution.py:52
  85.7 6.4 %all-to-all-start.1 = ((bf16[64,24,1024]{2,1,0:T(8,128)(2,1)}), bf16[64,24,1024]{2,1,0:T(8,128)(2,1)}, u32[]{:S(2)}, u32[]{:S(2)}) async-start(bf16[64,24,1024]{2,1,0:T(8,128)(2,1)} %broadcast_select_fusion), calls=%async_computation.2 | async-start | bytes 6291456 | tf_op jit(solution)/shard_map/all_to_all | solution.py:51
  92.1 0.5 broadcast.122
  92.7 0.7 reduce.5
  93.4 0.1 eq.54
  93.5 0.0 copy-done.7
  93.5 1.8 fusion.5
  95.3 69.3 %all-to-all-done.1 = bf16[64,24,1024]{2,1,0:T(8,128)(2,1)} async-done(((bf16[64,24,1024]{2,1,0:T(8,128)(2,1)}), bf16[64,24,1024]{2,1,0:T(8,128)(2,1)}, u32[]{:S(2)}, u32[]{:S(2)}) %all-to-all-start.1) | async-done | bytes 3145760 | tf_op jit(solution)/shard_map/all_to_all | solution.py:51
  164.6 4.0 %multiply_reduce_fusion = f32[1536,64]{0,1:T(8,128)S(1)} fusion(bf16[1536,1024,1]{1,0,2:T(8,128)(2,1)} %bitcast.5, bf16[8,64,1024]{2,1,0:T(8,128)(2,1)} %param.13, f32[1536,8]{0,1:T(8,128)S(1)} %get-tuple-element.6), kind=kOutput, calls=%fused_computation.9 | convolution fusion | flops 1612087296 | bytes 4636672 | tf_op jit(solution)/shard_map/dot_general | solution.py:63
  168.7 0.1 pad_maximum_fusion
  168.7 20.7 %all-reduce.1 = bf16[1536,128]{0,1:T(8,128)(2,1)S(1)} all-reduce(f32[1536,128]{0,1:T(8,128)S(1)} %pad_maximum_fusion), channel_id=1, replica_groups=mesh['wide'=64,'narrow'=4] {'narrow'}, use_global_device_ids=true, to_apply=%region_8.9 | all-reduce | flops 196608 | bytes 1179648 | tf_op jit(solution)/shard_map/psum | solution.py:79
  189.5 4.7 %fusion = bf16[1536,1024]{1,0:T(8,128)(2,1)} fusion(bf16[8,64,1024]{2,1,0:T(8,128)(2,1)} %param.13, bf16[1536,64]{0,1:T(8,128)(2,1)S(1)} %get-tuple-element.4, bf16[1536,8]{0,1:T(8,128)(2,1)S(1)} %get-tuple-element.5), kind=kOutput, calls=%fused_computation.7 | convolution fusion | flops 1614544896 | bytes 4415488 | tf_op jit(solution)/shard_map/dot_general | solution.py:91
  194.2 0.0 copy-start.6
  194.2 12.4 %all-to-all-start.3 = ((bf16[64,24,1024]{2,1,0:T(8,128)(2,1)}), bf16[64,24,1024]{2,1,0:T(8,128)(2,1)}, u32[]{:S(2)}, u32[]{:S(2)}) async-start(bf16[64,24,1024]{2,1,0:T(8,128)(2,1)} %bitcast.59), calls=%async_computation.4 | async-start | bytes 6291456 | tf_op jit(solution)/shard_map/all_to_all | solution.py:93
  206.6 0.0 copy-start.4
  206.6 0.0 copy-start.5
  206.7 0.0 copy-done.6
  206.7 2.8 fusion.9
  209.5 0.0 copy-done.4
  209.5 0.0 copy-done.5
  209.5 5.4 %multiply_add_fusion = f32[8,64,1024]{2,1,0:T(8,128)} fusion(bf16[8,64,1024]{2,1,0:T(8,128)(2,1)} %param.15, bf16[8,64,1024]{2,1,0:T(8,128)(2,1)S(1)} %copy-done.5, f32[8,64,1024]{2,1,0:T(8,128)S(1)} %copy-done.4, bf16[1536,1024,1]{1,0,2:T(8,128)(2,1)} %bitcast.5, bf16[1536,64]{0,1:T(8,128)(2,1)S(1)} %get-tuple-element.4, ...), kind=kOutput, calls=%fused_computation.13 | convolution fusion | flops 1615069184 | bytes 9658368 | tf_op jit(solution)/shard_map/dot_general | solution.py:100
  214.9 64.2 %all-to-all-done.3 = bf16[64,24,1024]{2,1,0:T(8,128)(2,1)} async-done(((bf16[64,24,1024]{2,1,0:T(8,128)(2,1)}), bf16[64,24,1024]{2,1,0:T(8,128)(2,1)}, u32[]{:S(2)}, u32[]{:S(2)}) %all-to-all-start.3) | async-done | bytes 3145760 | tf_op jit(solution)/shard_map/all_to_all | solution.py:93
  279.1 5.0 %gather_fusion.3 = bf16[512,1024]{1,0:T(8,128)(2,1)S(1)} fusion(bf16[1536,1024]{1,0:T(8,128)(2,1)} %bitcast.11, s32[1024]{0:T(1024)S(1)} %pad_clamp_fusion.1), kind=kCustom, calls=%fused_computation.3 | custom fusion | bytes 2099200 | tf_op jit(solution)/shard_map/gather | solution.py:122
  284.1 0.0 reduce-scatter.2.cloned.1.call-done
  284.2 2.9 add_convert_fusion
  (13 shorter events, 0.1 us)
Async XLA Ops:
  7.2 1.6 copy-start
  7.2 277.0 %reduce-scatter.2.cloned.1.call-start = ((), (), s32[]{:S(2)}) async-start(), calls=%async_computation.5 | async-start | bytes 10485760 | tf_op jit(solution)/shard_map/reduce_scatter | solution.py:121
  14.2 0.7 copy-start.3
  21.5 23.2 %copy-start.2 = (bf16[512,256]{1,0:T(8,128)(2,1)S(1)}, bf16[512,256]{1,0:T(8,128)(2,1)}, u32[]{:S(2)}) copy-start(bf16[512,256]{1,0:T(8,128)(2,1)} %param.11) | copy-start | bytes 786436
  31.7 22.3 %all-to-all-start = ((s32[64,1,24]{2,1,0:T(1,128)}), s32[64,1,24]{2,1,0:T(1,128)S(1)}, u32[]{:S(2)}, u32[]{:S(2)}) async-start(s32[64,1,24]{2,1,0:T(1,128)} %bitcast.2), calls=%async_computation.1 | async-start | bytes 65536 | tf_op jit(solution)/shard_map/all_to_all | solution.py:53
  50.1 12.9 %copy-start.1 = (bf16[512,1024]{1,0:T(8,128)(2,1)S(1)}, bf16[512,1024]{1,0:T(8,128)(2,1)}, u32[]{:S(2)}) copy-start(bf16[512,1024]{1,0:T(8,128)(2,1)} %param.10) | copy-start | bytes 3145732
  54.0 31.7 %all-to-all-start.2 = ((bf16[64,24,256]{2,1,0:T(8,128)(2,1)}), bf16[64,24,256]{2,1,0:T(8,128)(2,1)}, u32[]{:S(2)}, u32[]{:S(2)}) async-start(bf16[64,24,256]{2,1,0:T(8,128)(2,1)} %broadcast_select_fusion.1), calls=%async_computation.3 | async-start | bytes 1572864 | tf_op jit(solution)/shard_map/all_to_all | solution.py:52
  72.3 21.2 %copy-start.7 = (bf16[8,64,256]{2,1,0:T(8,128)(2,1)S(1)}, bf16[8,64,256]{2,1,0:T(8,128)(2,1)}, u32[]{:S(2)}) copy-start(bf16[8,64,256]{2,1,0:T(8,128)(2,1)} %param.14) | copy-start | bytes 786436
  85.7 78.9 %all-to-all-start.1 = ((bf16[64,24,1024]{2,1,0:T(8,128)(2,1)}), bf16[64,24,1024]{2,1,0:T(8,128)(2,1)}, u32[]{:S(2)}, u32[]{:S(2)}) async-start(bf16[64,24,1024]{2,1,0:T(8,128)(2,1)} %broadcast_select_fusion), calls=%async_computation.2 | async-start | bytes 6291456 | tf_op jit(solution)/shard_map/all_to_all | solution.py:51
  194.2 12.5 %copy-start.6 = (f32[8,64,256]{2,1,0:T(8,128)S(1)}, f32[8,64,256]{2,1,0:T(8,128)}, u32[]{:S(2)}) copy-start(f32[8,64,256]{2,1,0:T(8,128)} %param.18) | copy-start | bytes 1572868
  194.2 84.9 %all-to-all-start.3 = ((bf16[64,24,1024]{2,1,0:T(8,128)(2,1)}), bf16[64,24,1024]{2,1,0:T(8,128)(2,1)}, u32[]{:S(2)}, u32[]{:S(2)}) async-start(bf16[64,24,1024]{2,1,0:T(8,128)(2,1)} %bitcast.59), calls=%async_computation.4 | async-start | bytes 6291456 | tf_op jit(solution)/shard_map/all_to_all | solution.py:93
  206.6 2.8 copy-start.4
  206.6 2.8 copy-start.5
Sparse Core Ops, SparseCore 0:
  14.4 86.9 reduce-scatter.1
where the time goes:
time: 295 us; the launch traced here: 294 us
  waiting for transfers between devices  148 us (50%)
  starting transfers between devices  40.8 us (14%)
  local copies, waits for them, and re-layouts  34.5 us (12%)
  matrix products  24.2 us (8%)
  blocking collectives  20.7 us (7%)
  between operations  14.3 us (5%)
  other arithmetic  10.8 us (4%)
    all_to_all x1, waiting for transfers between devices, on_device(): lax.all_to_all(send_x, 'wide', split_axis=0, concat_axis=0, tiled=True)  69.3 us
    all_to_all x1, waiting for transfers between devices, on_device(): lax.all_to_all(adapter_row_product.reshape(tenant_list, tenant_adapters,...  64.2 us
    psum x1, blocking collectives, on_device(): summed = lax.psum(jnp.concatenate([u_part, g_part], axis=1), 'narrow')  20.7 us
    all_to_all x1, waiting for transfers between devices, on_device(): lax.all_to_all(send_dy, 'wide', split_axis=0, concat_axis=0, tiled=True)  13.5 us
    all_to_all x1, starting transfers between devices, on_device(): lax.all_to_all(send_id, 'wide', split_axis=0, concat_axis=0, tiled=True)  13 us
    all_to_all x1, starting transfers between devices, on_device(): lax.all_to_all(adapter_row_product.reshape(tenant_list, tenant_adapters,...  12.4 us
    gather x1, local copies, waits for them, and re-layouts, on_device(): local_id[source]  9.48 us
    all_to_all x1, starting transfers between devices, on_device(): lax.all_to_all(send_dy, 'wide', split_axis=0, concat_axis=0, tiled=True)  9 us
  transfers between devices with their start and end apart: 5, of which 4 were waited for; matrix products, arithmetic and copies ran while one was open for 20% of the time, Pallas kernels for 0%

commit v1 on v0

v1 whole, which is shorter than its diff:
```python
import jax
import jax.numpy as jnp
from jax import lax
from jax.experimental import pallas as pl
from jax.experimental.pallas import tpu as pltpu
from jax.sharding import PartitionSpec as P

MESH = pl.DeviceIdType.MESH
BF = jnp.bfloat16
F32 = jnp.float32

adapter_scale = 2.0
anchor_penalty_weight = 20.0

OFFSET = (1, 7, 2, 6, 3, 5, 4, 0)
MIRROR = (1, 0, 3, 2, 5, 4, 6, 7)
OWN = 7
ZROWS = 96
ZMSG = 112
SLOTS = 24
XROWS = 2 * SLOTS
XMSG = 64
PROWS = 8 * XROWS


def iota(shape, dim):
    return lax.broadcasted_iota(jnp.int32, shape, dim)


def fiota(shape, dim):
    return iota(shape, dim).astype(F32)


def onehot(hit):
    return jnp.where(hit, 1.0, 0.0).astype(BF)


def nn(a, b):
    return jnp.dot(a, b, preferred_element_type=F32)


def nt(a, b):
    return lax.dot_general(a, b, (((1,), (1,)), ((), ())), preferred_element_type=F32)


def tn(a, b):
    return lax.dot_general(a, b, (((0,), (0,)), ((), ())), preferred_element_type=F32)


def remote(src, dst, send, recv, **where):
    return pltpu.make_async_remote_copy(
        src_ref=src, dst_ref=dst, send_sem=send, recv_sem=recv, device_id=where, device_id_type=MESH
    )


def kernel(
    idx_h, tok_h, cot_h, w_h, dn_h, up_h, pdn_h, pup_h, fd_h, fu_h,
    lig_h, dg_h, ug_h,
    idx_v, tok_v, cot_v, w_v, dn_v, up_v, pdn_v, pup_v, fd_v, fu_v,
    lig_v, dg_v, ug_v, acc,
    g_mat, gt_mat, zs_dy, zs_x, zr_dy, zr_x, zs_l, zr_l,
    p_mat, pt_mat, xs_dy, xs_x, xr_dy, xr_x, xs_l, xr_l,
    mask, spread, part, ring, low, part_u, ring_u, low_u,
    loc, zdy_s, zdy_r, zx_s, zx_r, zl_s, zl_r,
    xdy_s, xdy_r, xx_s, xx_r, xl_s, xl_r, y_s, y_r,
):
    wide = lax.axis_index("wide")
    y = lax.axis_index("narrow")
    z = wide // 8
    me = wide % 8

    def z_dev(offset):
        return lax.rem(z + offset, 8) * 8 + me

    bar = pltpu.get_barrier_semaphore()
    for k in range(1, 8):
        pl.semaphore_signal(bar, inc=1, device_id={"wide": z_dev(k)}, device_id_type=MESH)
        pl.semaphore_signal(
            bar, inc=1, device_id={"wide": z * 8 + lax.rem(me + k, 8)}, device_id_type=MESH
        )
    for k in range(1, 4):
        pl.semaphore_signal(bar, inc=1, device_id={"narrow": lax.rem(y + k, 4)}, device_id_type=MESH)

    local = [
        pltpu.make_async_copy(a, b, loc.at[i])
        for i, (a, b) in enumerate(
            [
                (idx_h, idx_v), (cot_h, cot_v.at[y]), (tok_h, tok_v), (up_h, up_v), (dn_h, dn_v),
                (w_h.at[pl.ds(pl.multiple_of(y * 1024, 1024), 1024)], w_v.at[y]),
                (pdn_h, pdn_v), (pup_h, pup_v), (fd_h, fd_v), (fu_h, fu_v),
            ]
        )
    ]
    for c in local:
        c.start()

    local[0].wait()
    hi = idx_v[...] >> 6
    code = ((idx_v[...] & 63) + 1).astype(F32)
    row = iota((8, 512), 0)
    off = jnp.where(row == 7, 0, jnp.where((row & 1) == 0, (row >> 1) + 1, 7 - (row >> 1)))
    hit = ((z + off) & 7) == hi
    rank = nn(onehot(hit), onehot(iota((512, 512), 0) < iota((512, 512), 1)))
    slot = jnp.sum(jnp.where(hit, rank + row.astype(F32) * ZROWS, 0.0), axis=0, keepdims=True)
    code16 = jnp.broadcast_to(code, (16, 512)).astype(BF)
    local[1].wait()
    for b in range(8):
        g_b = onehot(slot == fiota((ZROWS, 512), 0) + float(b * ZROWS))
        g_mat[b] = g_b
        zs_dy[b, :ZROWS, :] = nn(g_b, cot_v[y]).astype(BF)
        zs_dy[b, ZROWS:, :] = jnp.zeros((ZMSG - ZROWS, 256), BF)
        zs_dy[b, ZROWS:, :ZROWS] = nt(code16, g_b).astype(BF)

    pl.semaphore_wait(bar, 17)

    def z_copy(src, dst, send, recv, b):
        return remote(
            src.at[b], dst.at[MIRROR[b]], send.at[b], recv.at[MIRROR[b]], wide=z_dev(OFFSET[b])
        )

    def z_wait(dst, send, recv, m):
        remote(dst.at[m], dst.at[m], send.at[m], recv.at[m], wide=z_dev(1)).wait_recv()

    for b in range(7):
        z_copy(zs_dy, zr_dy, zdy_s, zdy_r, b).start()
    zr_dy[OWN] = zs_dy[OWN]
    local[2].wait()
    for b in range(7):
        zs_x[b] = nn(g_mat[b], tok_v[...]).astype(BF)
        z_copy(zs_x, zr_x, zx_s, zx_r, b).start()
    zr_x[OWN] = nn(g_mat[OWN], tok_v[...]).astype(BF)

    def x_start(src, dst, send, recv, p):
        def one(j, carry):
            d = lax.rem(me + j, 8)
            remote(
                src.at[p, d], dst.at[p, me], send.at[p, d], recv.at[p, me], wide=z * 8 + d
            ).start()
            return carry

        lax.fori_loop(1, 8, one, 0)
        dst[p, me] = src[p, me]

    def x_wait(dst, send, recv, p):
        def one(j, carry):
            d = lax.rem(me + j, 8)
            remote(
                dst.at[p, d], dst.at[p, d], send.at[p, d], recv.at[p, d], wide=z * 8 + d
            ).wait_recv()
            return carry

        lax.fori_loop(1, 8, one, 0)

    upper = onehot(iota((128, 128), 0) < iota((128, 128), 1))

    def repack_dy(p):
        packed = jnp.zeros((PROWS, 256), F32)
        for i in range(2):
            m = 2 * p + i
            if m != OWN:
                z_wait(zr_dy, zdy_s, zdy_r, m)
            codes = zr_dy[m, ZROWS:, :128]
            line = codes.astype(F32)[:8]
            o8 = fiota((8, 128), 0) * 8.0
            in_o = (line > o8) & (line < o8 + 9.0)
            place = nn(onehot(in_o), upper) + o8 * (XROWS / 8.0) + float(i * SLOTS + 1)
            place = jnp.sum(jnp.where(in_o, place, 0.0), axis=0, keepdims=True) - 1.0
            p_mat[m] = onehot(place[:, :ZROWS] == fiota((PROWS, ZROWS), 0))
            packed = packed + nn(p_mat[m], zr_dy[m, :ZROWS, :])
        xs_dy[p, :, :XROWS, :] = packed.astype(BF).reshape(8, XROWS, 256)
        for d in range(8):
            sent = jnp.zeros((16, XROWS), F32)
            for i in range(2):
                m = 2 * p + i
                sent = sent + nt(
                    zr_dy[m, ZROWS:, :ZROWS], p_mat[m, d * XROWS : (d + 1) * XROWS, :]
                )
            xs_dy[p, d, XROWS:, :] = jnp.zeros((XMSG - XROWS, 256), BF)
            xs_dy[p, d, XROWS:, :XROWS] = sent.astype(BF)
        x_start(xs_dy, xr_dy, xdy_s, xdy_r, p)

    def repack_x(p):
        for i in range(2):
            if 2 * p + i != OWN:
                z_wait(zr_x, zx_s, zx_r, 2 * p + i)
        packed = nn(p_mat[2 * p], zr_x[2 * p]) + nn(p_mat[2 * p + 1], zr_x[2 * p + 1])
        xs_x[p] = packed.astype(BF).reshape(8, XROWS, 1024)
        x_start(xs_x, xr_x, xx_s, xx_r, p)

    for p in range(4):
        repack_dy(p)

    def fold(every, p):
        kept = every * mask[p].astype(F32)
        total = (kept[:, :128] + kept[:, 128:256]) + (kept[:, 256:384] + kept[:, 384:])
        return total + pltpu.roll(total, 64, 1)

    left = iota((PROWS, 128), 1) < 64

    def dy_rows(p):
        return xr_dy[p, :, :XROWS, :].reshape(PROWS, 256)

    def sum_start(halves, source, dst, n):
        source[0:2] = jnp.where(left, halves[0], halves[2]).reshape(2, 192, 128)
        source[2:4] = jnp.where(left, halves[1], halves[3]).reshape(2, 192, 128)
        for k in range(1, 4):
            t = lax.rem(y + k, 4)
            remote(source.at[t], dst.at[y], y_s.at[n, t], y_r.at[n, y], narrow=t).start()
        dst[y] = source[y]

    def y_wait(dst, n):
        for k in range(1, 4):
            t = lax.rem(y + k, 4)
            remote(dst.at[t], dst.at[t], y_s.at[n, t], y_r.at[n, t], narrow=t).wait_recv()

    def y_share(buf, n):
        for k in range(1, 4):
            t = lax.rem(y + k, 4)
            remote(buf.at[y], buf.at[y], y_s.at[n, t], y_r.at[n, y], narrow=t).start()

    def sum_share(src, dst, n):
        y_wait(src, n)
        dst[y] = ((src[0] + src[1]) + (src[2] + src[3])).astype(BF)
        y_share(dst, n + 1)

    def spread_of(buf, p):
        first = 2 * (p % 2)
        value = buf[first : first + 2].reshape(PROWS, 128).astype(F32)
        other = pltpu.roll(value, 64, 1)
        both = jnp.where(left, value, other) if p < 2 else jnp.where(left, other, value)
        return jnp.concatenate([both.astype(BF)] * 4, axis=1) * mask[p]

    def project_dy(p):
        x_wait(xr_dy, xdy_s, xdy_r, p)
        codes = xr_dy[p, :, XROWS:, :128].reshape(128, 128)
        pick = onehot(lax.rem(iota((PROWS, 128), 0), XROWS) == iota((PROWS, 128), 1))
        seen = nt(pick, codes)
        seen = jnp.where((iota((PROWS, 128), 0) // XROWS) * 16 == iota((PROWS, 128), 1), seen, 0.0)
        seen = jnp.sum(seen, axis=1, keepdims=True)
        wanted = (iota((PROWS, 512), 1) // 64 + (1 + 8 * me)).astype(F32)
        mask[p] = onehot(seen == wanted)
        return fold(nt(dy_rows(p), up_v[...]), p)

    repack_x(0)
    local[3].wait()
    halves = [project_dy(p) for p in range(4)]
    sum_start(halves, part, ring, 0)
    repack_x(1)
    sum_share(ring, low, 0)
    for k in range(1, 4):
        t = lax.rem(y + k, 4)
        remote(cot_v.at[y], cot_v.at[y], y_s.at[4, t], y_r.at[4, y], narrow=t).start()
        remote(
            w_h.at[pl.ds(pl.multiple_of(t * 1024, 1024), 1024)],
            w_v.at[y], y_s.at[5, t], y_r.at[5, y], narrow=t,
        ).start()
    local[4].wait()
    y_wait(low, 1)
    for p in range(4):
        spread[p] = spread_of(low, p)
        xs_l[p] = (adapter_scale * nn(spread[p], dn_v[...])).astype(BF).reshape(8, XROWS, 1024)
        x_start(xs_l, xr_l, xl_s, xl_r, p)
    repack_x(2)
    repack_x(3)

    for i in range(6, 10):
        local[i].wait()

    def penalty_down(i, carry):
        at = pl.ds(pl.multiple_of(i * 64, 64), 64)
        delta = dn_v[at, :].astype(F32) - pdn_v[at, :].astype(F32)
        dg_v[at, :] = anchor_penalty_weight * fd_v[at, :] * delta
        return carry

    lax.fori_loop(0, 8, penalty_down, 0)
    ug_v[...] = anchor_penalty_weight * fu_v[...] * (up_v[...].astype(F32) - pup_v[...].astype(F32))

    hi16 = jnp.broadcast_to(hi, (16, 512)).astype(F32).astype(BF)
    eye = onehot(iota((512, 512), 0) == iota((512, 512), 1))
    hi_col = nt(eye, hi16)[:, :1]
    lane = iota((512, 128), 1)
    off = jnp.where(lane == 7, 0, jnp.where((lane & 1) == 0, (lane >> 1) + 1, 7 - (lane >> 1)))
    hit = (((z + off) & 7).astype(F32) == hi_col) & (lane < 8)
    rank = nn(onehot(iota((512, 512), 0) > iota((512, 512), 1)), onehot(hit))
    slot_col = jnp.sum(
        jnp.where(hit, rank + lane.astype(F32) * ZROWS, 0.0), axis=1, keepdims=True
    )
    for p in range(4):
        gt_mat[p] = onehot(slot_col == fiota((512, 2 * ZROWS), 1) + float(p * 2 * ZROWS))

    def unpack(p):
        for i in range(2):
            codes = zr_dy[2 * p + i, ZROWS:, :128]
            col = nt(onehot(iota((ZROWS, 128), 0) == iota((ZROWS, 128), 1)), codes)[:, :1]
            o8 = fiota((ZROWS, 128), 1) * 8.0
            in_o = (col > o8) & (col < o8 + 9.0) & (o8 < 64.0)
            place = nn(onehot(iota((ZROWS, ZROWS), 0) > iota((ZROWS, ZROWS), 1)), onehot(in_o))
            place = place + o8 * (XROWS / 8.0) + float(i * SLOTS + 1)
            place = jnp.sum(jnp.where(in_o, place, 0.0), axis=1, keepdims=True) - 1.0
            pt_mat[i * ZROWS : (i + 1) * ZROWS, :] = onehot(place == fiota((ZROWS, PROWS), 1))
        x_wait(xr_l, xl_s, xl_r, p)
        rows = nn(pt_mat[...], xr_l[p].reshape(PROWS, 1024)).astype(BF)
        for i in range(2):
            m = 2 * p + i
            if m == OWN:
                zr_l[OWN] = rows[i * ZROWS : (i + 1) * ZROWS]
            else:
                zs_l[m] = rows[i * ZROWS : (i + 1) * ZROWS]
                z_copy(zs_l, zr_l, zl_s, zl_r, m).start()

    for p in range(4):
        unpack(p)

    y_wait(cot_v, 4)
    local[5].wait()
    y_wait(w_v, 5)

    def frozen(i, carry):
        at = pl.ds(pl.multiple_of(i * 128, 128), 128)
        total = nt(cot_v[0, at, :], w_v[0])
        for j in range(1, 4):
            total = total + nt(cot_v[j, at, :], w_v[j])
        acc[at, :] = total
        return carry

    lax.fori_loop(0, 4, frozen, 0)

    halves = []
    for p in range(4):
        x_wait(xr_x, xx_s, xx_r, p)
        rows = xr_x[p].reshape(PROWS, 1024)
        halves.append(fold(nt(rows, dn_v[...]), p))
        dg_v[...] += adapter_scale * tn(spread[p], rows)
    sum_start(halves, part_u, ring_u, 2)
    dg_copy = pltpu.make_async_copy(dg_v, dg_h, loc.at[10])
    dg_copy.start()
    sum_share(ring_u, low_u, 2)
    y_wait(low_u, 3)
    for p in range(4):
        ug_v[...] += adapter_scale * tn(spread_of(low_u, p), dy_rows(p))
    ug_copy = pltpu.make_async_copy(ug_v, ug_h, loc.at[11])
    ug_copy.start()

    for p in range(4):
        for i in range(2):
            if 2 * p + i != OWN:
                z_wait(zr_l, zl_s, zl_r, 2 * p + i)
        back = zr_l[2 * p : 2 * p + 2].reshape(2 * ZROWS, 1024)
        if p < 3:
            acc[...] += nn(gt_mat[p], back)
        else:
            lig_v[...] = (acc[...] + nn(gt_mat[p], back)).astype(BF)
    lig_copy = pltpu.make_async_copy(lig_v, lig_h, loc.at[12])
    lig_copy.start()

    for b in range(7):
        z_copy(zs_dy, zr_dy, zdy_s, zdy_r, b).wait_send()
        z_copy(zs_x, zr_x, zx_s, zx_r, b).wait_send()
        z_copy(zs_l, zr_l, zl_s, zl_r, b).wait_send()

    def x_sent(src, send, recv):
        def one(n, carry):
            p, d = n // 7, lax.rem(me + 1 + lax.rem(n, 7), 8)
            remote(
                src.at[p, d], src.at[p, d], send.at[p, d], recv.at[p, d], wide=z * 8 + d
            ).wait_send()
            return carry

        lax.fori_loop(0, 28, one, 0)

    x_sent(xs_dy, xdy_s, xdy_r)
    x_sent(xs_x, xx_s, xx_r)
    x_sent(xs_l, xl_s, xl_r)
    for n, buf in enumerate((ring, low, ring_u, low_u, cot_v, w_v)):
        for k in range(1, 4):
            t = lax.rem(y + k, 4)
            remote(buf.at[t], buf.at[t], y_s.at[n, t], y_r.at[n, t], narrow=t).wait_send()
    dg_copy.wait()
    ug_copy.wait()
    lig_copy.wait()


def on_device(
    tokens,
    cotangent,
    frozen_key_weight,
    adapter_down_maps,
    adapter_up_maps,
    previous_down_maps,
    previous_up_maps,
    down_fisher_diagonal,
    up_fisher_diagonal,
    token_adapter_index,
):
    vmem = pltpu.VMEM
    dma = pltpu.SemaphoreType.DMA
    scratch = [
        vmem((1, 512), jnp.int32), vmem((512, 1024), BF), vmem((4, 512, 256), BF), vmem((4, 1024, 256), BF),
        vmem((512, 1024), BF), vmem((512, 256), BF), vmem((512, 1024), BF), vmem((512, 256), BF),
        vmem((512, 1024), F32), vmem((512, 256), F32),
        vmem((512, 1024), BF), vmem((512, 1024), F32), vmem((512, 256), F32), vmem((512, 1024), F32),
        vmem((8, ZROWS, 512), BF), vmem((4, 512, 2 * ZROWS), BF),
        vmem((8, ZMSG, 256), BF), vmem((8, ZROWS, 1024), BF),
        vmem((8, ZMSG, 256), BF), vmem((8, ZROWS, 1024), BF),
        vmem((8, ZROWS, 1024), BF), vmem((8, ZROWS, 1024), BF),
        vmem((8, PROWS, ZROWS), BF), vmem((2 * ZROWS, PROWS), BF),
        vmem((4, 8, XMSG, 256), BF), vmem((4, 8, XROWS, 1024), BF),
        vmem((4, 8, XMSG, 256), BF), vmem((4, 8, XROWS, 1024), BF),
        vmem((4, 8, XROWS, 1024), BF), vmem((4, 8, XROWS, 1024), BF),
        vmem((4, PROWS, 512), BF), vmem((4, PROWS, 512), BF),
        vmem((4, 192, 128), F32), vmem((4, 192, 128), F32), vmem((4, 192, 128), BF),
        vmem((4, 192, 128), F32), vmem((4, 192, 128), F32), vmem((4, 192, 128), BF),
        dma((13,)), dma((8,)), dma((8,)), dma((8,)), dma((8,)), dma((8,)), dma((8,)),
        dma((4, 8)), dma((4, 8)), dma((4, 8)), dma((4, 8)), dma((4, 8)), dma((4, 8)),
        dma((6, 4)), dma((6, 4)),
    ]
    flat = lambda a: a.reshape(512, -1)
    lig, dg, ug = pl.pallas_call(
        kernel,
        out_shape=(
            jax.ShapeDtypeStruct((512, 1024), BF),
            jax.ShapeDtypeStruct((512, 1024), F32),
            jax.ShapeDtypeStruct((512, 256), F32),
        ),
        in_specs=[pl.BlockSpec(memory_space=pl.ANY)] * 10,
        out_specs=[pl.BlockSpec(memory_space=pl.ANY)] * 3,
        scratch_shapes=scratch,
        compiler_params=pltpu.CompilerParams(
            collective_id=0, has_side_effects=True, vmem_limit_bytes=60 * 1024 * 1024
        ),
        cost_estimate=pl.CostEstimate(flops=12_000_000_000, bytes_accessed=12_000_000, transcendentals=0),
    )(
        token_adapter_index.reshape(1, 512),
        tokens,
        cotangent,
        frozen_key_weight,
        flat(adapter_down_maps),
        flat(adapter_up_maps),
        flat(previous_down_maps),
        flat(previous_up_maps),
        flat(down_fisher_diagonal),
        flat(up_fisher_diagonal),
    )
    return lig, dg.reshape(adapter_down_maps.shape), ug.reshape(adapter_up_maps.shape)


def solution(mesh):
    in_specs = (
        P("wide", "narrow"),
        P("wide", "narrow"),
        P(None, "narrow"),
        P("wide", None, "narrow"),
        P("wide", None, "narrow"),
        P("wide", None, "narrow"),
        P("wide", None, "narrow"),
        P("wide", None, "narrow"),
        P("wide", None, "narrow"),
        P("wide"),
    )
    out_specs = (P("wide", "narrow"), P("wide", None, "narrow"), P("wide", None, "narrow"))
    return jax.shard_map(
        on_device, mesh=mesh, in_specs=in_specs, out_specs=out_specs, check_vma=False
    )
```

time: 295 us -> 131 us (0.44)
  the two profiles are of different devices: /device:TPU:1 before, /device:TPU:37 now
where the time goes in v1:
time: 131 us
  Pallas kernels  125 us (95%)
  local copies, waits for them, and re-layouts  4.6 us (4%)
    pallas_call x1, Pallas kernels, on_device(): pl.pallas_call(kernel, out_shape=(jax.ShapeDtypeStruct((512, 1024), BF),...  125 us
    unnamed x7, local copies, waits for them, and re-layouts  4.6 us

profile of v1, /device:TPU:37, one launch (start us, length us, event | category | flops | bytes accessed | tf_op | source)
XLA Modules:
  0.0 130.7 jit_solution(9544722105066202578)
XLA Ops:
  0.6 125.5 %shard_map.121 = (bf16[512,1024]{1,0:T(8,128)(2,1)}, f32[512,1024]{1,0:T(8,128)}, f32[512,256]{1,0:T(8,128)}) custom-call(s32[1,512]{1,0:T(1,128)} %bitcast.17, bf16[512,1024]{1,0:T(8,128)(2,1)} %tok_h.1, bf16[512,256]{1,0:T(8,128)(2,1)} %cot_h.1, bf16[4096,256]{1,0:T(8,128)(2,1)} %w_h.1, bf16[512,1024]{1,0:T(8,128)(2,1)} %bitcast.12, ...), custom_call_target="tpu_custom_call" | custom-call | flops 12000000000 | bytes 12000000 | tf_op jit(solution)/shard_map/pallas_call | solution.py:418
  126.1 0.0 copy-start
  126.1 2.4 %copy.16 = bf16[512,1024]{1,0:T(8,128)(2,1)} copy(bf16[512,1024]{1,0:T(8,128)(2,1)} %get-tuple-element.12) | data formatting | bytes 2097152
  128.5 0.0 copy-done
  128.5 0.0 copy-start.1
  128.5 1.3 %copy.17 = f32[8,64,1024]{2,1,0:T(8,128)} copy(f32[8,64,1024]{2,1,0:T(8,128)S(1)} %bitcast.9) | data formatting | bytes 4194304
  129.9 0.1 copy-done.1
  129.9 0.8 copy.18
Async XLA Ops:
  126.1 2.4 %copy-start = (f32[512,1024]{1,0:T(8,128)S(1)}, f32[512,1024]{1,0:T(8,128)}, u32[]{:S(2)}) copy-start(f32[512,1024]{1,0:T(8,128)} %get-tuple-element.7) | copy-start | bytes 6291460
  128.5 1.4 %copy-start.1 = (f32[512,256]{1,0:T(8,128)S(1)}, f32[512,256]{1,0:T(8,128)}, u32[]{:S(2)}) copy-start(f32[512,256]{1,0:T(8,128)} %get-tuple-element.8) | copy-start | bytes 1572868

commit v2 on v1

v2 whole, which is shorter than its diff:
```python
import jax
import jax.numpy as jnp
from jax import lax
from jax.experimental import pallas as pl
from jax.experimental.pallas import tpu as pltpu
from jax.sharding import PartitionSpec as P

MESH = pl.DeviceIdType.MESH
BF = jnp.bfloat16
F32 = jnp.float32

adapter_scale = 2.0
anchor_penalty_weight = 20.0

OFFSET = (1, 7, 2, 6, 3, 5, 4, 0)
MIRROR = (1, 0, 3, 2, 5, 4, 6, 7)
OWN = 7
ZROWS = 96
ZALL = 8 * ZROWS
SLOTS = 34
PACK = 8 * SLOTS
ROWS = 4 * PACK
HALF = 576
QUARTER = 144
COLS = 256
CHUNKS = 4


def iota(shape, dim):
    return lax.broadcasted_iota(jnp.int32, shape, dim)


def fiota(shape, dim):
    return iota(shape, dim).astype(F32)


def onehot(hit):
    return jnp.where(hit, 1.0, 0.0).astype(BF)


def nn(a, b):
    return jnp.dot(a, b, preferred_element_type=F32)


def nt(a, b):
    return lax.dot_general(a, b, (((1,), (1,)), ((), ())), preferred_element_type=F32)


def tn(a, b):
    return lax.dot_general(a, b, (((0,), (0,)), ((), ())), preferred_element_type=F32)


def remote(src, dst, send, recv, **where):
    return pltpu.make_async_remote_copy(
        src_ref=src, dst_ref=dst, send_sem=send, recv_sem=recv, device_id=where, device_id_type=MESH
    )


def offset_at(block):
    half = block >> 1
    return jnp.where(block == OWN, 0, jnp.where((block & 1) == 0, half + 1, 7 - half))


def kernel(
    idx_h, tok_h, cot_h, w_h, dn_h, up_h, pdn_h, pup_h, fd_h, fu_h,
    lig_h, dg_h, ug_h,
    idx_v, tok_v, cot_v, w_v, dn_v, up_v, pdn_v, pup_v, fd_v, fu_v,
    lig_v, dg_v, ug_v, acc,
    g_mat, gt_mat, p_mat, pt_mat,
    zs, zr, zs_c, zr_c, xs, xr, xs_c, xr_c, ls, lr, zs_l, zr_l,
    mask, spread, spread_u, part, ring, low, part_u, ring_u, low_u,
    dgs, dgr, ugs, ugr,
    loc, z_s, z_r, zc_s, zc_r, zl_s, zl_r, x_s, x_r, xc_s, xc_r, xl_s, xl_r, y_s, y_r, c_s, c_r,
):
    wide = lax.axis_index("wide")
    y = lax.axis_index("narrow")
    z = wide // 8
    me = wide % 8
    x = me // 2
    core = me % 2
    twin = wide + 1 - 2 * core

    def z_dev(offset):
        return lax.rem(z + offset, 8) * 8 + me

    def x_at(k):
        return lax.rem(x + k, 4)

    def x_dev(t):
        return z * 8 + t * 2 + core

    bar = pltpu.get_barrier_semaphore()
    for k in range(1, 8):
        pl.semaphore_signal(bar, inc=1, device_id={"wide": z_dev(k)}, device_id_type=MESH)
    for k in range(1, 4):
        pl.semaphore_signal(bar, inc=1, device_id={"wide": x_dev(x_at(k))}, device_id_type=MESH)
        pl.semaphore_signal(bar, inc=1, device_id={"narrow": lax.rem(y + k, 4)}, device_id_type=MESH)
    pl.semaphore_signal(bar, inc=1, device_id={"wide": twin}, device_id_type=MESH)

    local = [
        pltpu.make_async_copy(a, b, loc.at[i])
        for i, (a, b) in enumerate(
            [
                (idx_h, idx_v), (cot_h, cot_v.at[y]), (tok_h, tok_v), (up_h, up_v.at[core]), (dn_h, dn_v.at[core]),
                (w_h.at[pl.ds(pl.multiple_of(y * 1024, 1024), 1024)], w_v.at[y]),
                (pdn_h, pdn_v), (pup_h, pup_v), (fd_h, fd_v), (fu_h, fu_v),
            ]
        )
    ]
    for c in local:
        c.start()

    local[0].wait()
    hi = idx_v[...] >> 6
    code = ((idx_v[...] & 63) + 1).astype(F32)
    row = iota((8, 512), 0)
    hit = ((z + offset_at(row)) & 7) == hi
    rank = nn(onehot(hit), onehot(iota((512, 512), 0) < iota((512, 512), 1)))
    slot = jnp.sum(jnp.where(hit, rank + row.astype(F32) * ZROWS, 0.0), axis=0, keepdims=True)
    g_mat[...] = onehot(slot == fiota((ZALL, 512), 0))
    code16 = jnp.broadcast_to(code, (16, 512)).astype(BF)
    for b in range(8):
        sent = nt(code16, g_mat[b * ZROWS : (b + 1) * ZROWS, :])[:1]
        zs_c[b] = jnp.concatenate([sent, jnp.zeros((1, 128 - ZROWS), F32)], axis=1)
    local[1].wait()
    zs[0] = nn(g_mat[...], cot_v[y]).astype(BF).reshape(8, ZROWS, COLS)

    pl.semaphore_wait(bar, 14)

    def z_copy(src, dst, send, recv, b):
        return remote(src.at[b], dst.at[MIRROR[b]], send.at[b], recv.at[MIRROR[b]], wide=z_dev(OFFSET[b]))

    def z_start(src, dst, send, recv):
        for b in range(7):
            z_copy(src, dst, send, recv, b).start()
        dst[OWN] = src[OWN]

    def z_wait(dst, send, recv):
        for b in range(7):
            remote(dst.at[b], dst.at[b], send.at[b], recv.at[b], wide=z_dev(OFFSET[b])).wait_recv()

    def z_sent(src, send, recv):
        for b in range(7):
            remote(src.at[b], src.at[b], send.at[b], recv.at[b], wide=z_dev(OFFSET[b])).wait_send()

    def x_start(src, dst, send, recv):
        for k in range(1, 4):
            t = x_at(k)
            remote(src.at[t], dst.at[x], send.at[t], recv.at[x], wide=x_dev(t)).start()
        dst[x] = src[x]

    def x_wait(dst, send, recv):
        for k in range(1, 4):
            t = x_at(k)
            remote(dst.at[t], dst.at[t], send.at[t], recv.at[t], wide=x_dev(t)).wait_recv()

    def x_sent(src, send, recv):
        for k in range(1, 4):
            t = x_at(k)
            remote(src.at[t], src.at[t], send.at[t], recv.at[t], wide=x_dev(t)).wait_send()

    def to_twin(src, dst, n):
        return remote(src, dst, c_s.at[n], c_r.at[n], wide=twin)

    z_start(zs_c, zr_c, zc_s, zc_r)
    z_start(zs.at[0], zr.at[0], z_s.at[0], z_r.at[0])
    local[3].wait()
    local[4].wait()
    to_twin(up_v.at[core], up_v.at[core], 0).start()
    to_twin(dn_v.at[core], dn_v.at[core], 1).start()

    def y_share(buf, n):
        for k in range(1, 4):
            t = lax.rem(y + k, 4)
            remote(buf.at[y], buf.at[y], y_s.at[n, t], y_r.at[n, y], narrow=t).start()

    def y_wait(dst, n):
        for k in range(1, 4):
            t = lax.rem(y + k, 4)
            remote(dst.at[t], dst.at[t], y_s.at[n, t], y_r.at[n, t], narrow=t).wait_recv()

    y_share(cot_v, 4)
    local[2].wait()
    for k in range(CHUNKS):
        packed = nn(g_mat[...], tok_v[:, k * COLS : (k + 1) * COLS])
        zs[1 + k] = packed.astype(BF).reshape(8, ZROWS, COLS)
        z_start(zs.at[1 + k], zr.at[1 + k], z_s.at[1 + k], z_r.at[1 + k])

    z_wait(zr_c, zc_s, zc_r)
    codes = zr_c[:, 0, :]
    upper = onehot(iota((128, 128), 0) < iota((128, 128), 1))
    place = jnp.zeros((8, 128), F32)
    for t in range(4):
        inside = (codes > 16.0 * t) & (codes < 16.0 * t + 17.0)
        spot = nn(onehot(inside), upper) + fiota((8, 128), 0) * SLOTS + float(t * PACK + 1)
        place = place + jnp.where(inside, spot, 0.0)
    place = jnp.concatenate([place[m : m + 1, :ZROWS] for m in range(8)], axis=1) - 1.0
    p_mat[...] = onehot(place == fiota((ROWS, ZALL), 0))
    line = jnp.concatenate([codes[m : m + 1, :ZROWS] for m in range(8)], axis=1)
    line = jnp.broadcast_to(line, (16, ZALL)).astype(BF)
    for t in range(4):
        sent = nt(line, p_mat[t * PACK : (t + 1) * PACK, :])
        xs_c[t] = jnp.concatenate([sent, jnp.zeros((16, 384 - PACK), F32)], axis=1).astype(BF)
    x_start(xs_c, xr_c, xc_s, xc_r)

    def repack(k):
        z_wait(zr.at[k], z_s.at[k], z_r.at[k])
        xs[k] = nn(p_mat[...], zr[k].reshape(ZALL, COLS)).astype(BF).reshape(4, PACK, COLS)
        x_start(xs.at[k], xr.at[k], x_s.at[k], x_r.at[k])

    repack(0)

    codes32 = jnp.concatenate([jnp.broadcast_to(codes[m : m + 1], (4, 128)) for m in range(8)], axis=0)
    col = nt(onehot(iota((ZROWS, 128), 0) == iota((ZROWS, 128), 1)), codes32.astype(BF))
    lane = iota((ZROWS, 32), 1)
    first = (lane & 3).astype(F32) * 16.0
    inside = (col > first) & (col < first + 17.0)
    spot = nn(onehot(iota((ZROWS, ZROWS), 0) > iota((ZROWS, ZROWS), 1)), onehot(inside))
    spot = spot + ((lane & 3) * PACK + (lane >> 2) * SLOTS + 1).astype(F32)
    for m in range(8):
        at = jnp.sum(jnp.where(inside & ((lane >> 2) == m), spot, 0.0), axis=1, keepdims=True) - 1.0
        pt_mat[m * ZROWS : (m + 1) * ZROWS, :] = onehot(at == fiota((ZROWS, ROWS), 1))

    x_wait(xr_c, xc_s, xc_r)
    for t in range(4):
        seen = nt(onehot(iota((PACK, 384), 0) == iota((PACK, 384), 1)), xr_c[t])[:, :1]
        wanted = (iota((PACK, 1024), 1) // 64 + (1 + 16 * x)).astype(F32)
        mask[t] = onehot(seen == wanted)

    def fold(every, t):
        kept = every * mask[t].astype(F32)
        total = kept[:, :128]
        for j in range(1, 8):
            total = total + kept[:, j * 128 : (j + 1) * 128]
        return total + pltpu.roll(total, 64, 1)

    left = iota((HALF, 128), 1) < 64

    def sum_start(rows, source, dst, n):
        lower = jnp.concatenate([rows[HALF:], jnp.zeros((2 * HALF - ROWS, 128), F32)], axis=0)
        source[...] = jnp.where(left, rows[:HALF], lower).reshape(4, QUARTER, 128)
        for k in range(1, 4):
            t = lax.rem(y + k, 4)
            remote(source.at[t], dst.at[y], y_s.at[n, t], y_r.at[n, y], narrow=t).start()
        dst[y] = source[y]

    def sum_share(src, dst, n):
        y_wait(src, n)
        dst[y] = ((src[0] + src[1]) + (src[2] + src[3])).astype(BF)
        y_share(dst, n + 1)

    def spread_of(buf, out):
        value = buf[...].reshape(HALF, 128).astype(F32)
        other = pltpu.roll(value, 64, 1)
        high = jnp.where(left, value, other).astype(BF)
        rest = jnp.where(left, other, value).astype(BF)
        both = jnp.concatenate([high, rest[: ROWS - HALF]], axis=0)
        for t in range(4):
            one = jnp.concatenate([both[t * PACK : (t + 1) * PACK]] * 4, axis=1)
            for c in range(2):
                out[c, t * PACK : (t + 1) * PACK, :] = one * mask[t, :, c * 512 : (c + 1) * 512]

    to_twin(up_v.at[1 - core], up_v.at[1 - core], 0).wait_recv()
    x_wait(xr.at[0], x_s.at[0], x_r.at[0])
    up_all = up_v[...].reshape(1024, COLS)
    sum_start(
        jnp.concatenate([fold(nt(xr[0, t], up_all), t) for t in range(4)], axis=0), part, ring, 0
    )
    repack(1)
    sum_share(ring, low, 0)
    for k in range(1, 4):
        t = lax.rem(y + k, 4)
        remote(
            w_h.at[pl.ds(pl.multiple_of(t * 1024, 1024), 1024)],
            w_v.at[y], y_s.at[5, t], y_r.at[5, y], narrow=t,
        ).start()
    to_twin(dn_v.at[1 - core], dn_v.at[1 - core], 1).wait_recv()
    y_wait(low, 1)
    spread_of(low, spread)

    def lora(k):
        cols = slice(k * COLS, (k + 1) * COLS)
        rows = nn(spread[0], dn_v[0, :, cols]) + nn(spread[1], dn_v[1, :, cols])
        ls[k] = (adapter_scale * rows).astype(BF).reshape(4, PACK, COLS)
        x_start(ls.at[k], lr.at[k], xl_s.at[k], xl_r.at[k])

    def unpack(k):
        x_wait(lr.at[k], xl_s.at[k], xl_r.at[k])
        rows = nn(pt_mat[...], lr[k].reshape(ROWS, COLS)).astype(BF)
        zs_l[k] = rows.reshape(8, ZROWS, COLS)
        z_start(zs_l.at[k], zr_l.at[k], zl_s.at[k], zl_r.at[k])

    lora(0)
    repack(2)
    lora(1)
    lora(2)

    for i in range(6, 10):
        local[i].wait()

    def penalty_down(i, carry):
        at = pl.ds(pl.multiple_of(i * 64, 64), 64)
        delta = dn_v[core, at, :].astype(F32) - pdn_v[at, :].astype(F32)
        dg_v[at, :] = anchor_penalty_weight * fd_v[at, :] * delta
        return carry

    lax.fori_loop(0, 8, penalty_down, 0)
    delta = up_v[core].astype(F32) - pup_v[...].astype(F32)
    ug_v[...] = anchor_penalty_weight * fu_v[...] * delta

    unpack(0)
    repack(3)
    lora(3)
    unpack(1)
    repack(4)

    hi16 = jnp.broadcast_to(hi, (16, 512)).astype(F32).astype(BF)
    hi_col = nt(onehot(iota((512, 512), 0) == iota((512, 512), 1)), hi16)[:, :1]
    lane = iota((512, 128), 1)
    hit = (((z + offset_at(lane)) & 7).astype(F32) == hi_col) & (lane < 8)
    rank = nn(onehot(iota((512, 512), 0) > iota((512, 512), 1)), onehot(hit))
    slot_col = jnp.sum(jnp.where(hit, rank + lane.astype(F32) * ZROWS, 0.0), axis=1, keepdims=True)
    gt_mat[...] = onehot(slot_col == fiota((512, ZALL), 1))

    unpack(2)

    def gradient(k):
        x_wait(xr.at[k + 1], x_s.at[k + 1], x_r.at[k + 1])
        rows = xr[k + 1].reshape(ROWS, COLS)
        cols = slice(k * COLS, (k + 1) * COLS)
        dgs[k] = adapter_scale * tn(spread[1 - core], rows)
        to_twin(dgs.at[k], dgr.at[k], 2 + k).start()
        dg_v[:, cols] += adapter_scale * tn(spread[core], rows)

    gradient(0)
    gradient(1)
    unpack(3)
    gradient(2)
    gradient(3)

    def down_all(k):
        return dn_v[:, :, k * COLS : (k + 1) * COLS].reshape(1024, COLS)

    sums = []
    for t in range(4):
        every = nt(xr[1, t], down_all(0))
        for k in range(1, CHUNKS):
            every = every + nt(xr[1 + k, t], down_all(k))
        sums.append(fold(every, t))
    sum_start(jnp.concatenate(sums, axis=0), part_u, ring_u, 2)

    y_wait(cot_v, 4)
    local[5].wait()
    y_wait(w_v, 5)

    def frozen(i, carry):
        at = pl.ds(pl.multiple_of(i * 128, 128), 128)
        total = nt(cot_v[0, at, :], w_v[0])
        for j in range(1, 4):
            total = total + nt(cot_v[j, at, :], w_v[j])
        acc[at, :] = total
        return carry

    lax.fori_loop(0, 4, frozen, 0)

    sum_share(ring_u, low_u, 2)
    for k in range(CHUNKS):
        to_twin(dgr.at[k], dgr.at[k], 2 + k).wait_recv()
        dg_v[:, k * COLS : (k + 1) * COLS] += dgr[k]
    dg_copy = pltpu.make_async_copy(dg_v, dg_h, loc.at[10])
    dg_copy.start()
    y_wait(low_u, 3)
    spread_of(low_u, spread_u)
    ugs[...] = adapter_scale * tn(spread_u[1 - core], xr[0].reshape(ROWS, COLS))
    to_twin(ugs, ugr, 6).start()
    ug_v[...] += adapter_scale * tn(spread_u[core], xr[0].reshape(ROWS, COLS))

    def finish(k):
        cols = slice(k * COLS, (k + 1) * COLS)
        z_wait(zr_l.at[k], zl_s.at[k], zl_r.at[k])
        back = nn(gt_mat[...], zr_l[k].reshape(ZALL, COLS))
        lig_v[:, cols] = (acc[:, cols] + back).astype(BF)

    finish(0)
    finish(1)
    to_twin(ugr, ugr, 6).wait_recv()
    ug_v[...] += ugr[...]
    ug_copy = pltpu.make_async_copy(ug_v, ug_h, loc.at[11])
    ug_copy.start()
    finish(2)
    finish(3)
    lig_copy = pltpu.make_async_copy(lig_v, lig_h, loc.at[12])
    lig_copy.start()

    z_sent(zs_c, zc_s, zc_r)
    x_sent(xs_c, xc_s, xc_r)
    for k in range(1 + CHUNKS):
        z_sent(zs.at[k], z_s.at[k], z_r.at[k])
        x_sent(xs.at[k], x_s.at[k], x_r.at[k])
    for k in range(CHUNKS):
        z_sent(zs_l.at[k], zl_s.at[k], zl_r.at[k])
        x_sent(ls.at[k], xl_s.at[k], xl_r.at[k])
        to_twin(dgs.at[k], dgs.at[k], 2 + k).wait_send()
    to_twin(up_v.at[core], up_v.at[core], 0).wait_send()
    to_twin(dn_v.at[core], dn_v.at[core], 1).wait_send()
    to_twin(ugs, ugs, 6).wait_send()
    for n, buf in enumerate((ring, low, ring_u, low_u, cot_v, w_v)):
        for k in range(1, 4):
            t = lax.rem(y + k, 4)
            remote(buf.at[t], buf.at[t], y_s.at[n, t], y_r.at[n, t], narrow=t).wait_send()
    dg_copy.wait()
    ug_copy.wait()
    lig_copy.wait()


def on_device(
    tokens,
    cotangent,
    frozen_key_weight,
    adapter_down_maps,
    adapter_up_maps,
    previous_down_maps,
    previous_up_maps,
    down_fisher_diagonal,
    up_fisher_diagonal,
    token_adapter_index,
):
    vmem = pltpu.VMEM
    dma = pltpu.SemaphoreType.DMA
    scratch = [
        vmem((1, 512), jnp.int32), vmem((512, 1024), BF), vmem((4, 512, 256), BF), vmem((4, 1024, 256), BF),
        vmem((2, 512, 1024), BF), vmem((2, 512, 256), BF), vmem((512, 1024), BF), vmem((512, 256), BF),
        vmem((512, 1024), F32), vmem((512, 256), F32),
        vmem((512, 1024), BF), vmem((512, 1024), F32), vmem((512, 256), F32), vmem((512, 1024), F32),
        vmem((ZALL, 512), BF), vmem((512, ZALL), BF), vmem((ROWS, ZALL), BF), vmem((ZALL, ROWS), BF),
        vmem((5, 8, ZROWS, COLS), BF), vmem((5, 8, ZROWS, COLS), BF),
        vmem((8, 1, 128), F32), vmem((8, 1, 128), F32),
        vmem((5, 4, PACK, COLS), BF), vmem((5, 4, PACK, COLS), BF),
        vmem((4, 16, 384), BF), vmem((4, 16, 384), BF),
        vmem((4, 4, PACK, COLS), BF), vmem((4, 4, PACK, COLS), BF),
        vmem((4, 8, ZROWS, COLS), BF), vmem((4, 8, ZROWS, COLS), BF),
        vmem((4, PACK, 1024), BF), vmem((2, ROWS, 512), BF), vmem((2, ROWS, 512), BF),
        vmem((4, QUARTER, 128), F32), vmem((4, QUARTER, 128), F32), vmem((4, QUARTER, 128), BF),
        vmem((4, QUARTER, 128), F32), vmem((4, QUARTER, 128), F32), vmem((4, QUARTER, 128), BF),
        vmem((4, 512, COLS), F32), vmem((4, 512, COLS), F32), vmem((512, COLS), F32), vmem((512, COLS), F32),
        dma((13,)), dma((5, 8)), dma((5, 8)), dma((8,)), dma((8,)), dma((4, 8)), dma((4, 8)),
        dma((5, 4)), dma((5, 4)), dma((4,)), dma((4,)), dma((4, 4)), dma((4, 4)),
        dma((6, 4)), dma((6, 4)), dma((7,)), dma((7,)),
    ]
    flat = lambda a: a.reshape(512, -1)
    lig, dg, ug = pl.pallas_call(
        kernel,
        out_shape=(
            jax.ShapeDtypeStruct((512, 1024), BF),
            jax.ShapeDtypeStruct((512, 1024), F32),
            jax.ShapeDtypeStruct((512, 256), F32),
        ),
        in_specs=[pl.BlockSpec(memory_space=pl.ANY)] * 10,
        out_specs=[pl.BlockSpec(memory_space=pl.ANY)] * 3,
        scratch_shapes=scratch,
        compiler_params=pltpu.CompilerParams(
            collective_id=0, has_side_effects=True, vmem_limit_bytes=60 * 1024 * 1024
        ),
        cost_estimate=pl.CostEstimate(flops=12_000_000_000, bytes_accessed=12_000_000, transcendentals=0),
    )(
        token_adapter_index.reshape(1, 512),
        tokens,
        cotangent,
        frozen_key_weight,
        flat(adapter_down_maps),
        flat(adapter_up_maps),
        flat(previous_down_maps),
        flat(previous_up_maps),
        flat(down_fisher_diagonal),
        flat(up_fisher_diagonal),
    )
    return lig, dg.reshape(adapter_down_maps.shape), ug.reshape(adapter_up_maps.shape)


def solution(mesh):
    in_specs = (
        P("wide", "narrow"),
        P("wide", "narrow"),
        P(None, "narrow"),
        P("wide", None, "narrow"),
        P("wide", None, "narrow"),
        P("wide", None, "narrow"),
        P("wide", None, "narrow"),
        P("wide", None, "narrow"),
        P("wide", None, "narrow"),
        P("wide"),
    )
    out_specs = (P("wide", "narrow"), P("wide", None, "narrow"), P("wide", None, "narrow"))
    return jax.shard_map(
        on_device, mesh=mesh, in_specs=in_specs, out_specs=out_specs, check_vma=False
    )
```

time: 131 us -> 110 us (0.84)
  the two profiles are of different devices: /device:TPU:37 before, /device:TPU:1 now
where the time goes in v2:
time: 110 us
  Pallas kernels  104 us (95%)
  local copies, waits for them, and re-layouts  4.6 us (4%)
    pallas_call x1, Pallas kernels, on_device(): pl.pallas_call(kernel, out_shape=(jax.ShapeDtypeStruct((512, 1024), BF),...  104 us
    unnamed x7, local copies, waits for them, and re-layouts  4.6 us

profile of v2, /device:TPU:1, one launch (start us, length us, event | category | flops | bytes accessed | tf_op | source)
XLA Modules:
  0.0 109.6 jit_solution(4517587433100048326)
XLA Ops:
  0.6 104.4 %shard_map.121 = (bf16[512,1024]{1,0:T(8,128)(2,1)}, f32[512,1024]{1,0:T(8,128)}, f32[512,256]{1,0:T(8,128)}) custom-call(s32[1,512]{1,0:T(1,128)} %bitcast.17, bf16[512,1024]{1,0:T(8,128)(2,1)} %tok_h.1, bf16[512,256]{1,0:T(8,128)(2,1)} %cot_h.1, bf16[4096,256]{1,0:T(8,128)(2,1)} %w_h.1, bf16[512,1024]{1,0:T(8,128)(2,1)} %bitcast.12, ...), custom_call_target="tpu_custom_call" | custom-call | flops 12000000000 | bytes 12000000 | tf_op jit(solution)/shard_map/pallas_call | solution.py:451
  105.0 0.0 copy-start
  105.0 2.4 %copy.16 = bf16[512,1024]{1,0:T(8,128)(2,1)} copy(bf16[512,1024]{1,0:T(8,128)(2,1)} %get-tuple-element.12) | data formatting | bytes 2097152
  107.4 0.0 copy-done
  107.4 0.0 copy-start.1
  107.4 1.3 %copy.17 = f32[8,64,1024]{2,1,0:T(8,128)} copy(f32[8,64,1024]{2,1,0:T(8,128)S(1)} %bitcast.9) | data formatting | bytes 4194304
  108.8 0.1 copy-done.1
  108.8 0.8 copy.18
Async XLA Ops:
  105.0 2.4 %copy-start = (f32[512,1024]{1,0:T(8,128)S(1)}, f32[512,1024]{1,0:T(8,128)}, u32[]{:S(2)}) copy-start(f32[512,1024]{1,0:T(8,128)} %get-tuple-element.7) | copy-start | bytes 6291460
  107.4 1.4 %copy-start.1 = (f32[512,256]{1,0:T(8,128)S(1)}, f32[512,256]{1,0:T(8,128)}, u32[]{:S(2)}) copy-start(f32[512,256]{1,0:T(8,128)} %get-tuple-element.8) | copy-start | bytes 1572868

commit v3 on v2

--- a/solution.py
+++ b/solution.py
@@ -23,7 +23,10 @@
 HALF = 576
 QUARTER = 144
 COLS = 256
-CHUNKS = 4
+GRAD = ((0, 128), (128, 128))
+ND = len(GRAD)
+OUT = ((0, 256), (256, 256), (512, 256), (768, 256))
+BACK = ((0, 256), (256, 256), (512, 256), (768, 256))
 
 
 def iota(shape, dim):
@@ -69,8 +72,8 @@
     g_mat, gt_mat, p_mat, pt_mat,
     zs, zr, zs_c, zr_c, xs, xr, xs_c, xr_c, ls, lr, zs_l, zr_l,
     mask, spread, spread_u, part, ring, low, part_u, ring_u, low_u,
-    dgs, dgr, ugs, ugr,
-    loc, z_s, z_r, zc_s, zc_r, zl_s, zl_r, x_s, x_r, xc_s, xc_r, xl_s, xl_r, y_s, y_r, c_s, c_r,
+    dgs, dgr, held, xt, xt_c, mask_t,
+    loc, z_s, z_r, zc_s, zc_r, zl_s, zl_r, x_s, x_r, xc_s, xc_r, xl_s, xl_r, y_s, y_r, c_s, c_r, u_s, u_r,
 ):
     wide = lax.axis_index("wide")
     y = lax.axis_index("narrow")
@@ -94,7 +97,9 @@
         pl.semaphore_signal(bar, inc=1, device_id={"wide": z_dev(k)}, device_id_type=MESH)
     for k in range(1, 4):
         pl.semaphore_signal(bar, inc=1, device_id={"wide": x_dev(x_at(k))}, device_id_type=MESH)
-        pl.semaphore_signal(bar, inc=1, device_id={"narrow": lax.rem(y + k, 4)}, device_id_type=MESH)
+        t = lax.rem(y + k, 4)
+        pl.semaphore_signal(bar, inc=1, device_id={"narrow": t}, device_id_type=MESH)
+        pl.semaphore_signal(bar, inc=1, device_id={"wide": twin, "narrow": t}, device_id_type=MESH)
     pl.semaphore_signal(bar, inc=1, device_id={"wide": twin}, device_id_type=MESH)
 
     local = [
@@ -123,9 +128,11 @@
         sent = nt(code16, g_mat[b * ZROWS : (b + 1) * ZROWS, :])[:1]
         zs_c[b] = jnp.concatenate([sent, jnp.zeros((1, 128 - ZROWS), F32)], axis=1)
     local[1].wait()
-    zs[0] = nn(g_mat[...], cot_v[y]).astype(BF).reshape(8, ZROWS, COLS)
-
-    pl.semaphore_wait(bar, 14)
+    for k, (at, width) in enumerate(GRAD):
+        packed = nn(g_mat[...], cot_v[y, :, at : at + width])
+        zs[k][...] = packed.astype(BF).reshape(8, ZROWS, width)
+
+    pl.semaphore_wait(bar, 17)
 
     def z_copy(src, dst, send, recv, b):
         return remote(src.at[b], dst.at[MIRROR[b]], send.at[b], recv.at[MIRROR[b]], wide=z_dev(OFFSET[b]))
@@ -163,7 +170,8 @@
         return remote(src, dst, c_s.at[n], c_r.at[n], wide=twin)
 
     z_start(zs_c, zr_c, zc_s, zc_r)
-    z_start(zs.at[0], zr.at[0], z_s.at[0], z_r.at[0])
+    for k in range(ND):
+        z_start(zs[k], zr[k], z_s.at[k], z_r.at[k])
     local[3].wait()
     local[4].wait()
     to_twin(up_v.at[core], up_v.at[core], 0).start()
@@ -181,10 +189,10 @@
 
     y_share(cot_v, 4)
     local[2].wait()
-    for k in range(CHUNKS):
-        packed = nn(g_mat[...], tok_v[:, k * COLS : (k + 1) * COLS])
-        zs[1 + k] = packed.astype(BF).reshape(8, ZROWS, COLS)
-        z_start(zs.at[1 + k], zr.at[1 + k], z_s.at[1 + k], z_r.at[1 + k])
+    for k, (at, width) in enumerate(OUT, ND):
+        packed = nn(g_mat[...], tok_v[:, at : at + width])
+        zs[k][...] = packed.astype(BF).reshape(8, ZROWS, width)
+        z_start(zs[k], zr[k], z_s.at[k], z_r.at[k])
 
     z_wait(zr_c, zc_s, zc_r)
     codes = zr_c[:, 0, :]
@@ -204,11 +212,14 @@
     x_start(xs_c, xr_c, xc_s, xc_r)
 
     def repack(k):
-        z_wait(zr.at[k], z_s.at[k], z_r.at[k])
-        xs[k] = nn(p_mat[...], zr[k].reshape(ZALL, COLS)).astype(BF).reshape(4, PACK, COLS)
-        x_start(xs.at[k], xr.at[k], x_s.at[k], x_r.at[k])
-
-    repack(0)
+        width = zr[k].shape[2]
+        z_wait(zr[k], z_s.at[k], z_r.at[k])
+        rows = nn(p_mat[...], zr[k][...].reshape(ZALL, width))
+        xs[k][...] = rows.astype(BF).reshape(4, PACK, width)
+        x_start(xs[k], xr[k], x_s.at[k], x_r.at[k])
+
+    for k in range(ND):
+        repack(k)
 
     codes32 = jnp.concatenate([jnp.broadcast_to(codes[m : m + 1], (4, 128)) for m in range(8)], axis=0)
     col = nt(onehot(iota((ZROWS, 128), 0) == iota((ZROWS, 128), 1)), codes32.astype(BF))
@@ -221,11 +232,13 @@
         at = jnp.sum(jnp.where(inside & ((lane >> 2) == m), spot, 0.0), axis=1, keepdims=True) - 1.0
         pt_mat[m * ZROWS : (m + 1) * ZROWS, :] = onehot(at == fiota((ZROWS, ROWS), 1))
 
+    def named(codes, t, lanes, base):
+        seen = nt(onehot(iota((PACK, 384), 0) == iota((PACK, 384), 1)), codes[t])[:, :1]
+        return onehot(seen == (iota((PACK, lanes), 1) // 64 + base).astype(F32))
+
     x_wait(xr_c, xc_s, xc_r)
     for t in range(4):
-        seen = nt(onehot(iota((PACK, 384), 0) == iota((PACK, 384), 1)), xr_c[t])[:, :1]
-        wanted = (iota((PACK, 1024), 1) // 64 + (1 + 16 * x)).astype(F32)
-        mask[t] = onehot(seen == wanted)
+        mask[t] = named(xr_c, t, 1024, 1 + 16 * x)
 
     def fold(every, t):
         kept = every * mask[t].astype(F32)
@@ -236,6 +249,20 @@
 
     left = iota((HALF, 128), 1) < 64
 
+    def arrive(k):
+        x_wait(xr[k], x_s.at[k], x_r.at[k])
+
+    def rank_rows(maps, chunks, ks):
+        sums = []
+        for t in range(4):
+            every = None
+            for k in ks:
+                at, width = chunks[k] if chunks is GRAD else chunks[k - ND]
+                one = nt(xr[k][t], maps[:, :, at : at + width].reshape(1024, width))
+                every = one if every is None else every + one
+            sums.append(fold(every, t))
+        return jnp.concatenate(sums, axis=0)
+
     def sum_start(rows, source, dst, n):
         lower = jnp.concatenate([rows[HALF:], jnp.zeros((2 * HALF - ROWS, 128), F32)], axis=0)
         source[...] = jnp.where(left, rows[:HALF], lower).reshape(4, QUARTER, 128)
@@ -249,25 +276,30 @@
         dst[y] = ((src[0] + src[1]) + (src[2] + src[3])).astype(BF)
         y_share(dst, n + 1)
 
-    def spread_of(buf, out):
+    def rank_pairs(buf):
         value = buf[...].reshape(HALF, 128).astype(F32)
         other = pltpu.roll(value, 64, 1)
         high = jnp.where(left, value, other).astype(BF)
         rest = jnp.where(left, other, value).astype(BF)
-        both = jnp.concatenate([high, rest[: ROWS - HALF]], axis=0)
+        return jnp.concatenate([high, rest[: ROWS - HALF]], axis=0)
+
+    def spread_of(buf, out):
+        both = rank_pairs(buf)
         for t in range(4):
             one = jnp.concatenate([both[t * PACK : (t + 1) * PACK]] * 4, axis=1)
             for c in range(2):
                 out[c, t * PACK : (t + 1) * PACK, :] = one * mask[t, :, c * 512 : (c + 1) * 512]
 
     to_twin(up_v.at[1 - core], up_v.at[1 - core], 0).wait_recv()
-    x_wait(xr.at[0], x_s.at[0], x_r.at[0])
-    up_all = up_v[...].reshape(1024, COLS)
-    sum_start(
-        jnp.concatenate([fold(nt(xr[0, t], up_all), t) for t in range(4)], axis=0), part, ring, 0
-    )
-    repack(1)
+    repack(ND)
+    for k in range(ND):
+        arrive(k)
+    sum_start(rank_rows(up_v, GRAD, range(ND)), part, ring, 0)
+    for k in range(ND):
+        to_twin(xr[k], xt[k], 2 + k).start()
+    to_twin(xr_c, xt_c, 2 + ND).start()
     sum_share(ring, low, 0)
+    repack(ND + 1)
     for k in range(1, 4):
         t = lax.rem(y + k, 4)
         remote(
@@ -279,138 +311,188 @@
     spread_of(low, spread)
 
     def lora(k):
-        cols = slice(k * COLS, (k + 1) * COLS)
-        rows = nn(spread[0], dn_v[0, :, cols]) + nn(spread[1], dn_v[1, :, cols])
-        ls[k] = (adapter_scale * rows).astype(BF).reshape(4, PACK, COLS)
-        x_start(ls.at[k], lr.at[k], xl_s.at[k], xl_r.at[k])
+        at, width = BACK[k]
+        rows = nn(spread[0], dn_v[0, :, at : at + width])
+        rows = rows + nn(spread[1], dn_v[1, :, at : at + width])
+        ls[k][...] = (adapter_scale * rows).astype(BF).reshape(4, PACK, width)
+        x_start(ls[k], lr[k], xl_s.at[k], xl_r.at[k])
 
     def unpack(k):
-        x_wait(lr.at[k], xl_s.at[k], xl_r.at[k])
-        rows = nn(pt_mat[...], lr[k].reshape(ROWS, COLS)).astype(BF)
-        zs_l[k] = rows.reshape(8, ZROWS, COLS)
-        z_start(zs_l.at[k], zr_l.at[k], zl_s.at[k], zl_r.at[k])
+        width = BACK[k][1]
+        x_wait(lr[k], xl_s.at[k], xl_r.at[k])
+        rows = nn(pt_mat[...], lr[k][...].reshape(ROWS, width)).astype(BF)
+        zs_l[k][...] = rows.reshape(8, ZROWS, width)
+        z_start(zs_l[k], zr_l[k], zl_s.at[k], zl_r.at[k])
+
+    def penalties():
+        for i in range(6, 10):
+            local[i].wait()
+
+        def down(i, carry):
+            at = pl.ds(pl.multiple_of(i * 64, 64), 64)
+            delta = dn_v[core, at, :].astype(F32) - pdn_v[at, :].astype(F32)
+            dg_v[at, :] = anchor_penalty_weight * fd_v[at, :] * delta
+            return carry
+
+        lax.fori_loop(0, 8, down, 0)
+        delta = up_v[core].astype(F32) - pup_v[...].astype(F32)
+        ug_v[...] = anchor_penalty_weight * fu_v[...] * delta
+
+    def return_map():
+        hi16 = jnp.broadcast_to(hi, (16, 512)).astype(F32).astype(BF)
+        hi_col = nt(onehot(iota((512, 512), 0) == iota((512, 512), 1)), hi16)[:, :1]
+        lane = iota((512, 128), 1)
+        hit = (((z + offset_at(lane)) & 7).astype(F32) == hi_col) & (lane < 8)
+        rank = nn(onehot(iota((512, 512), 0) > iota((512, 512), 1)), onehot(hit))
+        slot_col = jnp.where(hit, rank + lane.astype(F32) * ZROWS, 0.0)
+        slot_col = jnp.sum(slot_col, axis=1, keepdims=True)
+        gt_mat[...] = onehot(slot_col == fiota((512, ZALL), 1))
+
+    def gradient(k):
+        at, width = OUT[k]
+        rows = xr[ND + k][...].reshape(ROWS, width)
+        dgs[k][...] = adapter_scale * tn(spread[1 - core], rows)
+        to_twin(dgs[k], dgr[k], 3 + ND + k).start()
+        dg_v[:, at : at + width] += adapter_scale * tn(spread[core], rows)
+
+    def frozen():
+        y_wait(cot_v, 4)
+        local[5].wait()
+        y_wait(w_v, 5)
+
+        def one(i, carry):
+            at = pl.ds(pl.multiple_of(i * 128, 128), 128)
+            total = nt(cot_v[0, at, :], w_v[0])
+            for j in range(1, 4):
+                total = total + nt(cot_v[j, at, :], w_v[j])
+            acc[at, :] = total
+            return carry
+
+        lax.fori_loop(0, 4, one, 0)
+
+    lig_copies = []
+
+    def finish(k):
+        at, width = BACK[k]
+        z_wait(zr_l[k], zl_s.at[k], zl_r.at[k])
+        back = nn(gt_mat[...], zr_l[k][...].reshape(ZALL, width))
+        lig_v[k][...] = (acc[:, at : at + width] + back).astype(BF)
+        lig_copies.append(
+            pltpu.make_async_copy(lig_v[k], lig_h.at[:, pl.ds(at, width)], loc.at[12 + k])
+        )
+        lig_copies[-1].start()
 
     lora(0)
-    repack(2)
     lora(1)
+    repack(ND + 2)
     lora(2)
-
-    for i in range(6, 10):
-        local[i].wait()
-
-    def penalty_down(i, carry):
-        at = pl.ds(pl.multiple_of(i * 64, 64), 64)
-        delta = dn_v[core, at, :].astype(F32) - pdn_v[at, :].astype(F32)
-        dg_v[at, :] = anchor_penalty_weight * fd_v[at, :] * delta
-        return carry
-
-    lax.fori_loop(0, 8, penalty_down, 0)
-    delta = up_v[core].astype(F32) - pup_v[...].astype(F32)
-    ug_v[...] = anchor_penalty_weight * fu_v[...] * delta
-
+    repack(ND + 3)
+    lora(3)
+    penalties()
     unpack(0)
-    repack(3)
-    lora(3)
+    return_map()
+    to_twin(xt_c, xt_c, 2 + ND).wait_recv()
+    for t in range(4):
+        mask_t[t] = named(xt_c, t, 512, 1 + 16 * x + 8 * core)
+    arrive(ND + 0)
+    gradient(0)
+    arrive(ND + 1)
+    gradient(1)
     unpack(1)
-    repack(4)
-
-    hi16 = jnp.broadcast_to(hi, (16, 512)).astype(F32).astype(BF)
-    hi_col = nt(onehot(iota((512, 512), 0) == iota((512, 512), 1)), hi16)[:, :1]
-    lane = iota((512, 128), 1)
-    hit = (((z + offset_at(lane)) & 7).astype(F32) == hi_col) & (lane < 8)
-    rank = nn(onehot(iota((512, 512), 0) > iota((512, 512), 1)), onehot(hit))
-    slot_col = jnp.sum(jnp.where(hit, rank + lane.astype(F32) * ZROWS, 0.0), axis=1, keepdims=True)
-    gt_mat[...] = onehot(slot_col == fiota((512, ZALL), 1))
-
+    frozen()
+    arrive(ND + 2)
+    gradient(2)
+    held[...] = rank_rows(dn_v, OUT, (ND, ND + 1, ND + 2))
     unpack(2)
-
-    def gradient(k):
-        x_wait(xr.at[k + 1], x_s.at[k + 1], x_r.at[k + 1])
-        rows = xr[k + 1].reshape(ROWS, COLS)
-        cols = slice(k * COLS, (k + 1) * COLS)
-        dgs[k] = adapter_scale * tn(spread[1 - core], rows)
-        to_twin(dgs.at[k], dgr.at[k], 2 + k).start()
-        dg_v[:, cols] += adapter_scale * tn(spread[core], rows)
-
-    gradient(0)
-    gradient(1)
+    arrive(ND + 3)
+    sum_start(held[...] + rank_rows(dn_v, OUT, (ND + 3,)), part_u, ring_u, 2)
     unpack(3)
-    gradient(2)
     gradient(3)
-
-    def down_all(k):
-        return dn_v[:, :, k * COLS : (k + 1) * COLS].reshape(1024, COLS)
-
-    sums = []
-    for t in range(4):
-        every = nt(xr[1, t], down_all(0))
-        for k in range(1, CHUNKS):
-            every = every + nt(xr[1 + k, t], down_all(k))
-        sums.append(fold(every, t))
-    sum_start(jnp.concatenate(sums, axis=0), part_u, ring_u, 2)
-
-    y_wait(cot_v, 4)
-    local[5].wait()
-    y_wait(w_v, 5)
-
-    def frozen(i, carry):
-        at = pl.ds(pl.multiple_of(i * 128, 128), 128)
-        total = nt(cot_v[0, at, :], w_v[0])
-        for j in range(1, 4):
-            total = total + nt(cot_v[j, at, :], w_v[j])
-        acc[at, :] = total
-        return carry
-
-    lax.fori_loop(0, 4, frozen, 0)
-
-    sum_share(ring_u, low_u, 2)
-    for k in range(CHUNKS):
-        to_twin(dgr.at[k], dgr.at[k], 2 + k).wait_recv()
-        dg_v[:, k * COLS : (k + 1) * COLS] += dgr[k]
+    y_wait(ring_u, 2)
+    low_u[core, y] = ((ring_u[0] + ring_u[1]) + (ring_u[2] + ring_u[3])).astype(BF)
+    for k in range(1, 4):
+        t = lax.rem(y + k, 4)
+        remote(low_u.at[core, y], low_u.at[core, y], y_s.at[3, t], y_r.at[3, y], narrow=t).start()
+    for k in range(4):
+        t = lax.rem(y + k, 4)
+        remote(
+            low_u.at[core, y], low_u.at[core, y], u_s.at[t], u_r.at[y], wide=twin, narrow=t
+        ).start()
+    finish(0)
+    for k, (at, width) in enumerate(OUT):
+        to_twin(dgr[k], dgr[k], 3 + ND + k).wait_recv()
+        dg_v[:, at : at + width] += dgr[k][...]
     dg_copy = pltpu.make_async_copy(dg_v, dg_h, loc.at[10])
     dg_copy.start()
-    y_wait(low_u, 3)
-    spread_of(low_u, spread_u)
-    ugs[...] = adapter_scale * tn(spread_u[1 - core], xr[0].reshape(ROWS, COLS))
-    to_twin(ugs, ugr, 6).start()
-    ug_v[...] += adapter_scale * tn(spread_u[core], xr[0].reshape(ROWS, COLS))
-
-    def finish(k):
-        cols = slice(k * COLS, (k + 1) * COLS)
-        z_wait(zr_l.at[k], zl_s.at[k], zl_r.at[k])
-        back = nn(gt_mat[...], zr_l[k].reshape(ZALL, COLS))
-        lig_v[:, cols] = (acc[:, cols] + back).astype(BF)
-
-    finish(0)
     finish(1)
-    to_twin(ugr, ugr, 6).wait_recv()
-    ug_v[...] += ugr[...]
+    for k in range(ND):
+        to_twin(xt[k], xt[k], 2 + k).wait_recv()
+    for k in range(1, 4):
+        t = lax.rem(y + k, 4)
+        remote(low_u.at[core, t], low_u.at[core, t], y_s.at[3, t], y_r.at[3, t], narrow=t).wait_recv()
+    for k in range(4):
+        t = lax.rem(y + k, 4)
+        remote(
+            low_u.at[1 - core, t], low_u.at[1 - core, t], u_s.at[t], u_r.at[t], wide=twin, narrow=t
+        ).wait_recv()
+    mine, theirs = rank_pairs(low_u.at[core]), rank_pairs(low_u.at[1 - core])
+    for t in range(4):
+        part_of = slice(t * PACK, (t + 1) * PACK)
+        wide_mask = jnp.where(core == 0, mask[t, :, :512], mask[t, :, 512:])
+        spread_u[0, part_of, :] = jnp.concatenate([mine[part_of]] * 4, axis=1) * wide_mask
+        spread_u[1, part_of, :] = jnp.concatenate([theirs[part_of]] * 4, axis=1) * mask_t[t]
+    for k, (at, width) in enumerate(GRAD):
+        both = tn(spread_u[0], xr[k][...].reshape(ROWS, width))
+        both = both + tn(spread_u[1], xt[k][...].reshape(ROWS, width))
+        ug_v[:, at : at + width] += adapter_scale * both
     ug_copy = pltpu.make_async_copy(ug_v, ug_h, loc.at[11])
     ug_copy.start()
-    finish(2)
-    finish(3)
-    lig_copy = pltpu.make_async_copy(lig_v, lig_h, loc.at[12])
-    lig_copy.start()
+    for k in range(2, len(BACK)):
+        finish(k)
 
     z_sent(zs_c, zc_s, zc_r)
     x_sent(xs_c, xc_s, xc_r)
-    for k in range(1 + CHUNKS):
-        z_sent(zs.at[k], z_s.at[k], z_r.at[k])
-        x_sent(xs.at[k], x_s.at[k], x_r.at[k])
-    for k in range(CHUNKS):
-        z_sent(zs_l.at[k], zl_s.at[k], zl_r.at[k])
-        x_sent(ls.at[k], xl_s.at[k], xl_r.at[k])
-        to_twin(dgs.at[k], dgs.at[k], 2 + k).wait_send()
+    for k in range(len(OUT) + ND):
+        z_sent(zs[k], z_s.at[k], z_r.at[k])
+        x_sent(xs[k], x_s.at[k], x_r.at[k])
+    for k in range(len(OUT)):
+        to_twin(dgs[k], dgs[k], 3 + ND + k).wait_send()
+    for k in range(ND):
+        to_twin(xr[k], xr[k], 2 + k).wait_send()
+    to_twin(xr_c, xr_c, 2 + ND).wait_send()
+    for k in range(len(BACK)):
+        z_sent(zs_l[k], zl_s.at[k], zl_r.at[k])
+        x_sent(ls[k], xl_s.at[k], xl_r.at[k])
     to_twin(up_v.at[core], up_v.at[core], 0).wait_send()
     to_twin(dn_v.at[core], dn_v.at[core], 1).wait_send()
-    to_twin(ugs, ugs, 6).wait_send()
-    for n, buf in enumerate((ring, low, ring_u, low_u, cot_v, w_v)):
+    for k in range(4):
+        t = lax.rem(y + k, 4)
+        remote(low_u.at[0, t], low_u.at[0, t], u_s.at[t], u_r.at[t], wide=twin, narrow=t).wait_send()
+    for n, buf in enumerate((ring, low, ring_u, low_u.at[0], cot_v, w_v)):
         for k in range(1, 4):
             t = lax.rem(y + k, 4)
             remote(buf.at[t], buf.at[t], y_s.at[n, t], y_r.at[n, t], narrow=t).wait_send()
     dg_copy.wait()
     ug_copy.wait()
-    lig_copy.wait()
+    for c in lig_copies:
+        c.wait()
+
+
+def deliver(lig, dg, ug, lig_out, dg_out, ug_out, lig_v, dg_v, ug_v, into, back):
+    inward, outward = [], []
+    for src, held, dst, parts in ((dg, dg_v, dg_out, 4), (lig, lig_v, lig_out, 2), (ug, ug_v, ug_out, 1)):
+        for i in range(parts):
+            at = pl.ds(i * (512 // parts), 512 // parts)
+            n = len(inward)
+            inward.append(pltpu.make_async_copy(src.at[at], held.at[at], into.at[n]))
+            outward.append(pltpu.make_async_copy(held.at[at], dst.at[at], back.at[n]))
+    for c in inward:
+        c.start()
+    for c, d in zip(inward, outward):
+        c.wait()
+        d.start()
+    for d in outward:
+        d.wait()
 
 
 def on_device(
@@ -427,25 +509,29 @@
 ):
     vmem = pltpu.VMEM
     dma = pltpu.SemaphoreType.DMA
+    no, nb = len(OUT) + ND, len(BACK)
+    RANKED = GRAD + OUT
+    each = lambda chunks, dims, kind: tuple(vmem((*dims, width), kind) for _, width in chunks)
     scratch = [
         vmem((1, 512), jnp.int32), vmem((512, 1024), BF), vmem((4, 512, 256), BF), vmem((4, 1024, 256), BF),
         vmem((2, 512, 1024), BF), vmem((2, 512, 256), BF), vmem((512, 1024), BF), vmem((512, 256), BF),
         vmem((512, 1024), F32), vmem((512, 256), F32),
-        vmem((512, 1024), BF), vmem((512, 1024), F32), vmem((512, 256), F32), vmem((512, 1024), F32),
+        each(BACK, (512,), BF), vmem((512, 1024), F32), vmem((512, 256), F32), vmem((512, 1024), F32),
         vmem((ZALL, 512), BF), vmem((512, ZALL), BF), vmem((ROWS, ZALL), BF), vmem((ZALL, ROWS), BF),
-        vmem((5, 8, ZROWS, COLS), BF), vmem((5, 8, ZROWS, COLS), BF),
+        each(RANKED, (8, ZROWS), BF), each(RANKED, (8, ZROWS), BF),
         vmem((8, 1, 128), F32), vmem((8, 1, 128), F32),
-        vmem((5, 4, PACK, COLS), BF), vmem((5, 4, PACK, COLS), BF),
+        each(RANKED, (4, PACK), BF), each(RANKED, (4, PACK), BF),
         vmem((4, 16, 384), BF), vmem((4, 16, 384), BF),
-        vmem((4, 4, PACK, COLS), BF), vmem((4, 4, PACK, COLS), BF),
-        vmem((4, 8, ZROWS, COLS), BF), vmem((4, 8, ZROWS, COLS), BF),
+        each(BACK, (4, PACK), BF), each(BACK, (4, PACK), BF),
+        each(BACK, (8, ZROWS), BF), each(BACK, (8, ZROWS), BF),
         vmem((4, PACK, 1024), BF), vmem((2, ROWS, 512), BF), vmem((2, ROWS, 512), BF),
         vmem((4, QUARTER, 128), F32), vmem((4, QUARTER, 128), F32), vmem((4, QUARTER, 128), BF),
-        vmem((4, QUARTER, 128), F32), vmem((4, QUARTER, 128), F32), vmem((4, QUARTER, 128), BF),
-        vmem((4, 512, COLS), F32), vmem((4, 512, COLS), F32), vmem((512, COLS), F32), vmem((512, COLS), F32),
-        dma((13,)), dma((5, 8)), dma((5, 8)), dma((8,)), dma((8,)), dma((4, 8)), dma((4, 8)),
-        dma((5, 4)), dma((5, 4)), dma((4,)), dma((4,)), dma((4, 4)), dma((4, 4)),
-        dma((6, 4)), dma((6, 4)), dma((7,)), dma((7,)),
+        vmem((4, QUARTER, 128), F32), vmem((4, QUARTER, 128), F32), vmem((2, 4, QUARTER, 128), BF),
+        each(OUT, (512,), F32), each(OUT, (512,), F32),
+        vmem((ROWS, 128), F32), each(GRAD, (4, PACK), BF), vmem((4, 16, 384), BF), vmem((4, PACK, 512), BF),
+        dma((12 + nb,)), dma((no, 8)), dma((no, 8)), dma((8,)), dma((8,)), dma((nb, 8)), dma((nb, 8)),
+        dma((no, 4)), dma((no, 4)), dma((4,)), dma((4,)), dma((nb, 4)), dma((nb, 4)),
+        dma((6, 4)), dma((6, 4)), dma((3 + no,)), dma((3 + no,)), dma((4,)), dma((4,)),
     ]
     flat = lambda a: a.reshape(512, -1)
     lig, dg, ug = pl.pallas_call(
@@ -474,6 +560,16 @@
         flat(down_fisher_diagonal),
         flat(up_fisher_diagonal),
     )
+    whole = pl.BlockSpec(memory_space=pl.ANY)
+    lig, dg, ug = pl.pallas_call(
+        deliver,
+        out_shape=tuple(jax.ShapeDtypeStruct(a.shape, a.dtype) for a in (lig, dg, ug)),
+        in_specs=[whole] * 3,
+        out_specs=[whole] * 3,
+        scratch_shapes=[vmem(a.shape, a.dtype) for a in (lig, dg, ug)] + [dma((7,)), dma((7,))],
+        compiler_params=pltpu.CompilerParams(vmem_limit_bytes=60 * 1024 * 1024),
+        cost_estimate=pl.CostEstimate(flops=0, bytes_accessed=7_340_032, transcendentals=0),
+    )(lig, dg, ug)
     return lig, dg.reshape(adapter_down_maps.shape), ug.reshape(adapter_up_maps.shape)
 
 

time: 110 us -> 102 us (0.927)
  local copies, waits for them, and re-layouts: 4.6 us -> 0 us
  Pallas kernels: 104 us -> 101 us
    pallas_call x1, Pallas kernels: 104 us -> 98.1 us  [on_device(): pl.pallas_call(kernel, out_shape=(jax.ShapeDtypeStruct((512, 1024), BF),...]
    unnamed x7 -> x0, local copies, waits for them, and re-layouts: 4.6 us -> none
    pallas_call x0 -> x1, Pallas kernels: none -> 3.02 us  [on_device(): pl.pallas_call(deliver, out_shape=tuple((jax.ShapeDtypeStruct(a.shape, a....]
where the time goes in v3:
time: 102 us
  Pallas kernels  101 us (99%)
    pallas_call x1, Pallas kernels, on_device(): pl.pallas_call(kernel, out_shape=(jax.ShapeDtypeStruct((512, 1024), BF),...  98.1 us
    pallas_call x1, Pallas kernels, on_device(): pl.pallas_call(deliver, out_shape=tuple((jax.ShapeDtypeStruct(a.shape, a....  3.02 us

profile of v3, /device:TPU:1, one launch (start us, length us, event | category | flops | bytes accessed | tf_op | source)
XLA Modules:
  0.0 101.9 jit_solution(8158589281508959204)
XLA Ops:
  0.6 98.1 %shard_map.121 = (bf16[512,1024]{1,0:T(8,128)(2,1)}, f32[512,1024]{1,0:T(8,128)}, f32[512,256]{1,0:T(8,128)}) custom-call(s32[1,512]{1,0:T(1,128)} %bitcast.17, bf16[512,1024]{1,0:T(8,128)(2,1)} %tok_h.1, bf16[512,256]{1,0:T(8,128)(2,1)} %cot_h.1, bf16[4096,256]{1,0:T(8,128)(2,1)} %w_h.1, bf16[512,1024]{1,0:T(8,128)(2,1)} %bitcast.11, ...), custom_call_target="tpu_custom_call" | custom-call | flops 12000000000 | bytes 12000000 | tf_op jit(solution)/shard_map/pallas_call | solution.py:537
  98.7 3.0 %shard_map.122 = (bf16[512,1024]{1,0:T(8,128)(2,1)}, f32[512,1024]{1,0:T(8,128)}, f32[512,256]{1,0:T(8,128)}) custom-call(bf16[512,1024]{1,0:T(8,128)(2,1)} %get-tuple-element.9.lig, f32[512,1024]{1,0:T(8,128)} %get-tuple-element.10.dg, f32[512,256]{1,0:T(8,128)} %get-tuple-element.11.ug), custom_call_target="tpu_custom_call" | custom-call | bytes 7340032 | tf_op jit(solution)/shard_map/pallas_call | solution.py:564

commit v4 on v3

--- a/solution.py
+++ b/solution.py
@@ -66,15 +66,16 @@
 
 def kernel(
     idx_h, tok_h, cot_h, w_h, dn_h, up_h, pdn_h, pup_h, fd_h, fu_h,
-    lig_h, dg_h, ug_h,
+    lig_0, lig_1, lig_2, lig_3, dg_v, ug_v,
     idx_v, tok_v, cot_v, w_v, dn_v, up_v, pdn_v, pup_v, fd_v, fu_v,
-    lig_v, dg_v, ug_v, acc,
+    acc,
     g_mat, gt_mat, p_mat, pt_mat,
     zs, zr, zs_c, zr_c, xs, xr, xs_c, xr_c, ls, lr, zs_l, zr_l,
     mask, spread, spread_u, part, ring, low, part_u, ring_u, low_u,
     dgs, dgr, held, xt, xt_c, mask_t,
     loc, z_s, z_r, zc_s, zc_r, zl_s, zl_r, x_s, x_r, xc_s, xc_r, xl_s, xl_r, y_s, y_r, c_s, c_r, u_s, u_r,
 ):
+    lig_v = (lig_0, lig_1, lig_2, lig_3)
     wide = lax.axis_index("wide")
     y = lax.axis_index("narrow")
     z = wide // 8
@@ -306,24 +307,6 @@
             w_h.at[pl.ds(pl.multiple_of(t * 1024, 1024), 1024)],
             w_v.at[y], y_s.at[5, t], y_r.at[5, y], narrow=t,
         ).start()
-    to_twin(dn_v.at[1 - core], dn_v.at[1 - core], 1).wait_recv()
-    y_wait(low, 1)
-    spread_of(low, spread)
-
-    def lora(k):
-        at, width = BACK[k]
-        rows = nn(spread[0], dn_v[0, :, at : at + width])
-        rows = rows + nn(spread[1], dn_v[1, :, at : at + width])
-        ls[k][...] = (adapter_scale * rows).astype(BF).reshape(4, PACK, width)
-        x_start(ls[k], lr[k], xl_s.at[k], xl_r.at[k])
-
-    def unpack(k):
-        width = BACK[k][1]
-        x_wait(lr[k], xl_s.at[k], xl_r.at[k])
-        rows = nn(pt_mat[...], lr[k][...].reshape(ROWS, width)).astype(BF)
-        zs_l[k][...] = rows.reshape(8, ZROWS, width)
-        z_start(zs_l[k], zr_l[k], zl_s.at[k], zl_r.at[k])
-
     def penalties():
         for i in range(6, 10):
             local[i].wait()
@@ -348,6 +331,29 @@
         slot_col = jnp.sum(slot_col, axis=1, keepdims=True)
         gt_mat[...] = onehot(slot_col == fiota((512, ZALL), 1))
 
+    penalties()
+    return_map()
+    to_twin(xt_c, xt_c, 2 + ND).wait_recv()
+    for t in range(4):
+        mask_t[t] = named(xt_c, t, 512, 1 + 16 * x + 8 * core)
+    to_twin(dn_v.at[1 - core], dn_v.at[1 - core], 1).wait_recv()
+    y_wait(low, 1)
+    spread_of(low, spread)
+
+    def lora(k):
+        at, width = BACK[k]
+        rows = nn(spread[0], dn_v[0, :, at : at + width])
+        rows = rows + nn(spread[1], dn_v[1, :, at : at + width])
+        ls[k][...] = (adapter_scale * rows).astype(BF).reshape(4, PACK, width)
+        x_start(ls[k], lr[k], xl_s.at[k], xl_r.at[k])
+
+    def unpack(k):
+        width = BACK[k][1]
+        x_wait(lr[k], xl_s.at[k], xl_r.at[k])
+        rows = nn(pt_mat[...], lr[k][...].reshape(ROWS, width)).astype(BF)
+        zs_l[k][...] = rows.reshape(8, ZROWS, width)
+        z_start(zs_l[k], zr_l[k], zl_s.at[k], zl_r.at[k])
+
     def gradient(k):
         at, width = OUT[k]
         rows = xr[ND + k][...].reshape(ROWS, width)
@@ -370,39 +376,30 @@
 
         lax.fori_loop(0, 4, one, 0)
 
-    lig_copies = []
 
     def finish(k):
         at, width = BACK[k]
         z_wait(zr_l[k], zl_s.at[k], zl_r.at[k])
         back = nn(gt_mat[...], zr_l[k][...].reshape(ZALL, width))
         lig_v[k][...] = (acc[:, at : at + width] + back).astype(BF)
-        lig_copies.append(
-            pltpu.make_async_copy(lig_v[k], lig_h.at[:, pl.ds(at, width)], loc.at[12 + k])
-        )
-        lig_copies[-1].start()
 
     lora(0)
     lora(1)
     repack(ND + 2)
     lora(2)
-    repack(ND + 3)
-    lora(3)
-    penalties()
-    unpack(0)
-    return_map()
-    to_twin(xt_c, xt_c, 2 + ND).wait_recv()
-    for t in range(4):
-        mask_t[t] = named(xt_c, t, 512, 1 + 16 * x + 8 * core)
     arrive(ND + 0)
     gradient(0)
     arrive(ND + 1)
     gradient(1)
+    repack(ND + 3)
+    lora(3)
+    unpack(0)
+    held[...] = rank_rows(dn_v, OUT, (ND, ND + 1))
     unpack(1)
     frozen()
     arrive(ND + 2)
     gradient(2)
-    held[...] = rank_rows(dn_v, OUT, (ND, ND + 1, ND + 2))
+    held[...] += rank_rows(dn_v, OUT, (ND + 2,))
     unpack(2)
     arrive(ND + 3)
     sum_start(held[...] + rank_rows(dn_v, OUT, (ND + 3,)), part_u, ring_u, 2)
@@ -422,8 +419,6 @@
     for k, (at, width) in enumerate(OUT):
         to_twin(dgr[k], dgr[k], 3 + ND + k).wait_recv()
         dg_v[:, at : at + width] += dgr[k][...]
-    dg_copy = pltpu.make_async_copy(dg_v, dg_h, loc.at[10])
-    dg_copy.start()
     finish(1)
     for k in range(ND):
         to_twin(xt[k], xt[k], 2 + k).wait_recv()
@@ -445,11 +440,8 @@
         both = tn(spread_u[0], xr[k][...].reshape(ROWS, width))
         both = both + tn(spread_u[1], xt[k][...].reshape(ROWS, width))
         ug_v[:, at : at + width] += adapter_scale * both
-    ug_copy = pltpu.make_async_copy(ug_v, ug_h, loc.at[11])
-    ug_copy.start()
-    for k in range(2, len(BACK)):
+    for k in range(2, len(BACK) - 1):
         finish(k)
-
     z_sent(zs_c, zc_s, zc_r)
     x_sent(xs_c, xc_s, xc_r)
     for k in range(len(OUT) + ND):
@@ -461,7 +453,8 @@
         to_twin(xr[k], xr[k], 2 + k).wait_send()
     to_twin(xr_c, xr_c, 2 + ND).wait_send()
     for k in range(len(BACK)):
-        z_sent(zs_l[k], zl_s.at[k], zl_r.at[k])
+        if k < len(BACK) - 1:
+            z_sent(zs_l[k], zl_s.at[k], zl_r.at[k])
         x_sent(ls[k], xl_s.at[k], xl_r.at[k])
     to_twin(up_v.at[core], up_v.at[core], 0).wait_send()
     to_twin(dn_v.at[core], dn_v.at[core], 1).wait_send()
@@ -472,27 +465,21 @@
         for k in range(1, 4):
             t = lax.rem(y + k, 4)
             remote(buf.at[t], buf.at[t], y_s.at[n, t], y_r.at[n, t], narrow=t).wait_send()
-    dg_copy.wait()
-    ug_copy.wait()
-    for c in lig_copies:
+    finish(len(BACK) - 1)
+    z_sent(zs_l[len(BACK) - 1], zl_s.at[len(BACK) - 1], zl_r.at[len(BACK) - 1])
+
+
+def deliver(*refs):
+    nb = len(BACK)
+    *lig, dg, ug = refs[: nb + 2]
+    lig_out, dg_out, ug_out, sem = refs[nb + 2 :]
+    copies = [pltpu.make_async_copy(dg, dg_out, sem.at[nb]), pltpu.make_async_copy(ug, ug_out, sem.at[nb + 1])]
+    for k, (at, width) in enumerate(BACK):
+        copies.append(pltpu.make_async_copy(lig[k], lig_out.at[:, pl.ds(at, width)], sem.at[k]))
+    for c in copies:
+        c.start()
+    for c in copies:
         c.wait()
-
-
-def deliver(lig, dg, ug, lig_out, dg_out, ug_out, lig_v, dg_v, ug_v, into, back):
-    inward, outward = [], []
-    for src, held, dst, parts in ((dg, dg_v, dg_out, 4), (lig, lig_v, lig_out, 2), (ug, ug_v, ug_out, 1)):
-        for i in range(parts):
-            at = pl.ds(i * (512 // parts), 512 // parts)
-            n = len(inward)
-            inward.append(pltpu.make_async_copy(src.at[at], held.at[at], into.at[n]))
-            outward.append(pltpu.make_async_copy(held.at[at], dst.at[at], back.at[n]))
-    for c in inward:
-        c.start()
-    for c, d in zip(inward, outward):
-        c.wait()
-        d.start()
-    for d in outward:
-        d.wait()
 
 
 def on_device(
@@ -516,7 +503,7 @@
         vmem((1, 512), jnp.int32), vmem((512, 1024), BF), vmem((4, 512, 256), BF), vmem((4, 1024, 256), BF),
         vmem((2, 512, 1024), BF), vmem((2, 512, 256), BF), vmem((512, 1024), BF), vmem((512, 256), BF),
         vmem((512, 1024), F32), vmem((512, 256), F32),
-        each(BACK, (512,), BF), vmem((512, 1024), F32), vmem((512, 256), F32), vmem((512, 1024), F32),
+        vmem((512, 1024), F32),
         vmem((ZALL, 512), BF), vmem((512, ZALL), BF), vmem((ROWS, ZALL), BF), vmem((ZALL, ROWS), BF),
         each(RANKED, (8, ZROWS), BF), each(RANKED, (8, ZROWS), BF),
         vmem((8, 1, 128), F32), vmem((8, 1, 128), F32),
@@ -534,18 +521,18 @@
         dma((6, 4)), dma((6, 4)), dma((3 + no,)), dma((3 + no,)), dma((4,)), dma((4,)),
     ]
     flat = lambda a: a.reshape(512, -1)
-    lig, dg, ug = pl.pallas_call(
+    *lig, dg, ug = pl.pallas_call(
         kernel,
         out_shape=(
-            jax.ShapeDtypeStruct((512, 1024), BF),
-            jax.ShapeDtypeStruct((512, 1024), F32),
-            jax.ShapeDtypeStruct((512, 256), F32),
+            *(pltpu.VMEM((512, width), BF) for _, width in BACK),
+            pltpu.VMEM((512, 1024), F32),
+            pltpu.VMEM((512, 256), F32),
         ),
         in_specs=[pl.BlockSpec(memory_space=pl.ANY)] * 10,
-        out_specs=[pl.BlockSpec(memory_space=pl.ANY)] * 3,
+        out_specs=[pl.BlockSpec(memory_space=pltpu.VMEM)] * (nb + 2),
         scratch_shapes=scratch,
         compiler_params=pltpu.CompilerParams(
-            collective_id=0, has_side_effects=True, vmem_limit_bytes=60 * 1024 * 1024
+            collective_id=0, has_side_effects=True, vmem_limit_bytes=56 * 1024 * 1024
         ),
         cost_estimate=pl.CostEstimate(flops=12_000_000_000, bytes_accessed=12_000_000, transcendentals=0),
     )(
@@ -560,16 +547,19 @@
         flat(down_fisher_diagonal),
         flat(up_fisher_diagonal),
     )
-    whole = pl.BlockSpec(memory_space=pl.ANY)
     lig, dg, ug = pl.pallas_call(
         deliver,
-        out_shape=tuple(jax.ShapeDtypeStruct(a.shape, a.dtype) for a in (lig, dg, ug)),
-        in_specs=[whole] * 3,
-        out_specs=[whole] * 3,
-        scratch_shapes=[vmem(a.shape, a.dtype) for a in (lig, dg, ug)] + [dma((7,)), dma((7,))],
-        compiler_params=pltpu.CompilerParams(vmem_limit_bytes=60 * 1024 * 1024),
+        out_shape=(
+            jax.ShapeDtypeStruct((512, 1024), BF),
+            jax.ShapeDtypeStruct((512, 1024), F32),
+            jax.ShapeDtypeStruct((512, 256), F32),
+        ),
+        in_specs=[pl.BlockSpec(memory_space=pltpu.VMEM)] * (nb + 2),
+        out_specs=[pl.BlockSpec(memory_space=pl.ANY)] * 3,
+        scratch_shapes=[dma((nb + 2,))],
+        compiler_params=pltpu.CompilerParams(vmem_limit_bytes=1024 * 1024),
         cost_estimate=pl.CostEstimate(flops=0, bytes_accessed=7_340_032, transcendentals=0),
-    )(lig, dg, ug)
+    )(*(pltpu.with_memory_space_constraint(a, pltpu.VMEM) for a in (*lig, dg, ug)))
     return lig, dg.reshape(adapter_down_maps.shape), ug.reshape(adapter_up_maps.shape)
 
 

time: 102 us -> 99.8 us (0.978)
  Pallas kernels: 101 us -> 98.9 us
    pallas_call x2, Pallas kernels: 101 us -> 98.9 us  [the longest x1 97 us: on_device(): pl.pallas_call(kernel, out_shape=(*(pltpu.VMEM((512, width), BF) for _, w...]
where the time goes in v4:
time: 99.8 us; the launch traced here: 99.7 us
  Pallas kernels  98.9 us (99%)
    pallas_call x1, Pallas kernels, on_device(): pl.pallas_call(kernel, out_shape=(*(pltpu.VMEM((512, width), BF) for _, w...  97 us

profile of v4, /device:TPU:1, one launch (start us, length us, event | category | flops | bytes accessed | tf_op | source)
XLA Modules:
  0.0 99.7 jit_solution(11594623626495757117)
XLA Ops:
  0.6 97.0 %shard_map.121 = (bf16[512,256]{1,0:T(8,128)(2,1)S(1)}, bf16[512,256]{1,0:T(8,128)(2,1)S(1)}, bf16[512,256]{1,0:T(8,128)(2,1)S(1)}, bf16[512,256]{1,0:T(8,128)(2...) custom-call(s32[1,512]{1,0:T(1,128)} %bitcast.17, bf16[512,1024]{1,0:T(8,128)(2,1)} %tok_h.1, ...), custom_call_target="tpu_custom_call" | custom-call | flops 12000000000 | bytes 12000000 | tf_op jit(solution)/shard_map/pallas_call | solution.py:524
  97.6 1.9 %shard_map.122 = (bf16[512,1024]{1,0:T(8,128)(2,1)}, f32[512,1024]{1,0:T(8,128)}, f32[512,256]{1,0:T(8,128)}) custom-call(bf16[512,256]{1,0:T(8,128)(2,1)S(1)} %get-tuple-element.12.refs_0_, bf16[512,256]{1,0:T(8,128)(2,1)S(1)} %get-tuple-element.13.refs_1_, bf16[512,256]{1,0:T(8,128)(2,1)S(1)} %get-tuple-element.14.refs_2_, ...), custom_call_target="tpu_custom_call" | custom-call | bytes 7340032 | tf_op jit(solution)/shard_map/pallas_call | solution.py:550

commit v5 on v4

--- a/solution.py
+++ b/solution.py
@@ -396,11 +396,11 @@
     unpack(0)
     held[...] = rank_rows(dn_v, OUT, (ND, ND + 1))
     unpack(1)
-    frozen()
     arrive(ND + 2)
     gradient(2)
+    unpack(2)
+    frozen()
     held[...] += rank_rows(dn_v, OUT, (ND + 2,))
-    unpack(2)
     arrive(ND + 3)
     sum_start(held[...] + rank_rows(dn_v, OUT, (ND + 3,)), part_u, ring_u, 2)
     unpack(3)

time: 99.8 us -> 101 us (1.012)
  Pallas kernels: 98.9 us -> 100 us
    pallas_call x1, Pallas kernels: 97 us -> 98.1 us  [on_device(): pl.pallas_call(kernel, out_shape=(*(pltpu.VMEM((512, width), BF) for _, w...]
where the time goes in v5:
time: 101 us
  Pallas kernels  100 us (99%)
    pallas_call x1, Pallas kernels, on_device(): pl.pallas_call(kernel, out_shape=(*(pltpu.VMEM((512, width), BF) for _, w...  98.1 us

profile of v5, /device:TPU:1, one launch (start us, length us, event | category | flops | bytes accessed | tf_op | source)
XLA Modules:
  0.0 100.8 jit_solution(3003750033050189704)
XLA Ops:
  0.6 98.1 %shard_map.121 = (bf16[512,256]{1,0:T(8,128)(2,1)S(1)}, bf16[512,256]{1,0:T(8,128)(2,1)S(1)}, bf16[512,256]{1,0:T(8,128)(2,1)S(1)}, bf16[512,256]{1,0:T(8,128)(2...) custom-call(s32[1,512]{1,0:T(1,128)} %bitcast.17, bf16[512,1024]{1,0:T(8,128)(2,1)} %tok_h.1, ...), custom_call_target="tpu_custom_call" | custom-call | flops 12000000000 | bytes 12000000 | tf_op jit(solution)/shard_map/pallas_call | solution.py:524
  98.7 1.9 %shard_map.122 = (bf16[512,1024]{1,0:T(8,128)(2,1)}, f32[512,1024]{1,0:T(8,128)}, f32[512,256]{1,0:T(8,128)}) custom-call(bf16[512,256]{1,0:T(8,128)(2,1)S(1)} %get-tuple-element.12.refs_0_, bf16[512,256]{1,0:T(8,128)(2,1)S(1)} %get-tuple-element.13.refs_1_, bf16[512,256]{1,0:T(8,128)(2,1)S(1)} %get-tuple-element.14.refs_2_, ...), custom_call_target="tpu_custom_call" | custom-call | bytes 7340032 | tf_op jit(solution)/shard_map/pallas_call | solution.py:550
